TPU v7x, 32 devices: a whole 2x2x4 slice. The times are simulated.
32 devices in a mesh: item: 2 (over core), row: 4 (over y, x), col: 4 (over z).
Axes of the slice: x: 2, y: 2, z: 4, core: 2. Of those that a mesh axis runs over, the one named last changes fastest.
Arguments:
- latents: bfloat16 [2, 2, 16, 16, 3072], P('item', None, 'row', 'col'), may hold values from -640 to 640
- prompt_rows: bfloat16 [2, 226, 3072], P('item'), may hold values from -640 to 640
- peg_weight: bfloat16 [3, 3, 3072], replicated, may hold values from -1 to 1
- modulation_weight: bfloat16 [512, 6144], P(None, 'col'), may hold values from -0.5 to 0.5
- qkv_weight: bfloat16 [3072, 3, 2048], P(('item', 'row'), None, 'col'), may hold values from -3 to 3
- text_len: int32 [2], P('item'), may hold values from 56 to 226, as said below
- timestep: int32 [2], P('item'), may hold values from 0 to 999
Outputs:
- attended: bfloat16 [2, 2, 16, 16, 2048], P('item', None, 'row', None, 'col')
Inputs may be any that keep to these rules, and one draw needn't show every extreme that they name: `text_len`: one item has all 226 text tokens valid; the others have fewer.
All inputs are finite; a program needn't handle non-finite values.
Results may differ from a plain program's by a relative error of at most 0.02.
Values may be sent and summed in bfloat16 or wider, within the bound.
A program may use at most 64 MiB of HBM per device.

v0:
```python
import math

import jax
import jax.numpy as jnp
from jax import lax
from jax.sharding import PartitionSpec as P

HD = 64


def with_halo(block, sides, width):
    for axis, dim in sides:
        count = lax.axis_size(axis)
        forward = [(i, i + 1) for i in range(count - 1)]
        backward = [(target, source) for source, target in forward]
        low = lax.ppermute(
            lax.slice_in_dim(block, block.shape[dim] - width, None, axis=dim), axis, forward
        )
        high = lax.ppermute(lax.slice_in_dim(block, 0, width, axis=dim), axis, backward)
        block = jnp.concatenate([low, block, high], axis=dim)
    return block


def time_angles(step, count):
    half = count // 2
    freqs = jnp.exp(-math.log(10000.0) * jnp.arange(half, dtype=jnp.float32) / half)
    angle = step.astype(jnp.float32) * freqs
    return jnp.concatenate([jnp.cos(angle), jnp.sin(angle)])


def modulate(rows, shift, scale):
    values = rows.astype(jnp.float32)
    center = jnp.mean(values, axis=-1, keepdims=True)
    centered = values - center
    spread = jnp.mean(centered * centered, axis=-1, keepdims=True)
    return (centered * lax.rsqrt(spread + 1e-06) * (1.0 + scale) + shift).astype(jnp.bfloat16)


def absorb(carry, queries, key_rows, value_rows, valid):
    running_max, running_sum, weighted = carry
    count = key_rows.shape[0]
    heads = queries.shape[1]
    key_heads = key_rows.reshape(count, heads, HD)
    value_heads = value_rows.reshape(count, heads, HD)
    scores = (
        jnp.einsum("rhd,bhd->rhb", queries, key_heads, preferred_element_type=jnp.float32) * 0.125
    )
    if valid is not None:
        scores = jnp.where(valid[None, None, :], scores, -jnp.inf)
    newest = jnp.maximum(running_max, jnp.max(scores, axis=-1))
    weights = jnp.exp(scores - newest[..., None])
    shrink_by = jnp.exp(running_max - newest)
    running_sum = running_sum * shrink_by + jnp.sum(weights, axis=-1)
    weighted = weighted * shrink_by[..., None] + jnp.einsum(
        "rhb,bhd->rhd",
        weights.astype(jnp.bfloat16),
        value_heads,
        preferred_element_type=jnp.float32,
    )
    return (newest, running_sum, weighted)


def on_device(latents, prompt_rows, peg_weight, modulation_weight, qkv_weight, text_len, timestep):
    tile_h = latents.shape[2]
    tile_w = latents.shape[3]
    width = latents.shape[4]
    padded = with_halo(latents, (("row", 2), ("col", 3)), 1)
    summed = latents.astype(jnp.float32)
    for row_tap in range(3):
        for col_tap in range(3):
            summed = summed + padded[
                :, :, row_tap : row_tap + tile_h, col_tap : col_tap + tile_w, :
            ].astype(jnp.float32) * peg_weight[row_tap, col_tap].astype(jnp.float32)
    convolved = summed.astype(jnp.bfloat16)
    activation = jax.nn.silu(time_angles(timestep[0], modulation_weight.shape[0])).astype(
        jnp.bfloat16
    )
    own_columns = jnp.dot(
        activation[None, :], modulation_weight, preferred_element_type=jnp.float32
    )
    modulation = lax.all_gather(own_columns, "col", axis=1, tiled=True)[0]
    shift = modulation[:width]
    scale = modulation[width:]
    group_rows = lax.all_gather(modulate(convolved, shift, scale), "col", axis=3, tiled=True)
    frames = group_rows.shape[1]
    grid_w = group_rows.shape[3]
    flat_rows = group_rows.reshape(-1, width)
    row_count = flat_rows.shape[0]
    text_normed = modulate(prompt_rows[0], shift, scale)
    text_count = text_normed.shape[0]
    head_width = qkv_weight.shape[2]
    full_weight = lax.all_gather(qkv_weight, ("item", "row"), axis=0, tiled=True)
    latent_proj = jnp.einsum(
        "rd,dkc->rkc", flat_rows, full_weight, preferred_element_type=jnp.float32
    )
    text_proj = jnp.einsum(
        "rd,dkc->rkc", text_normed, full_weight, preferred_element_type=jnp.float32
    )
    latent_qkv = latent_proj.astype(jnp.bfloat16)
    text_qkv = text_proj.astype(jnp.bfloat16)
    heads = head_width // HD
    queries = latent_qkv[:, 0, :].reshape(row_count, heads, HD)
    local_keys = latent_qkv[:, 1, :]
    local_values = latent_qkv[:, 2, :]
    text_valid = jnp.arange(text_count, dtype=jnp.int32) < text_len[0]
    start_carry = (
        jnp.full((row_count, heads), -jnp.inf, jnp.float32),
        jnp.zeros((row_count, heads), jnp.float32),
        jnp.zeros((row_count, heads, HD), jnp.float32),
    )
    text_carry = absorb(start_carry, queries, text_qkv[:, 1, :], text_qkv[:, 2, :], text_valid)
    key_rows = lax.all_gather(local_keys, "row", axis=0, tiled=True)
    value_rows = lax.all_gather(local_values, "row", axis=0, tiled=True)
    total_rows = key_rows.shape[0]
    block_count = total_rows // row_count

    def one_block(state, pair):
        return (absorb(state, queries, pair[0], pair[1], None), None)

    state, unused = lax.scan(
        one_block,
        text_carry,
        (
            key_rows.reshape(block_count, row_count, head_width),
            value_rows.reshape(block_count, row_count, head_width),
        ),
    )
    running_max, running_sum, weighted = state
    attended = (weighted / running_sum[..., None]).astype(jnp.bfloat16)
    return attended.reshape(1, frames, tile_h, grid_w, head_width)


def solution(mesh):
    in_specs = (
        P("item", None, "row", "col", None),
        P("item", None, None),
        P(),
        P(None, "col"),
        P(("item", "row"), None, "col"),
        P("item"),
        P("item"),
    )
    out_specs = P("item", None, "row", None, "col")
    return jax.shard_map(
        on_device, mesh=mesh, in_specs=in_specs, out_specs=out_specs, check_vma=False
    )
```

profile of v0, /device:TPU:0, one launch (start us, length us, event | category | flops | bytes accessed | tf_op | source)
XLA Modules:
  0.0 123.0 jit_solution(7482106777228331044)
XLA Ops:
  6.5 0.7 all-gather.6.cloned.1.call-update
  7.3 1.2 copy.25
  8.5 0.8 fusion.53
  9.3 4.8 %collective-permute-start = (bf16[1,2,1,4,3072]{4,2,1,0,3:T(2,128)(2,1)}, bf16[1,2,1,4,3072]{4,2,1,0,3:T(2,128)(2,1)S(1)}, u32[]{:S(2)}, u32[]{:S(2)}) collective-permute-start(bf16[1,2,1,4,3072]{4,2,1,0,3:T(2,128)(2,1)} %get-tuple-element.97), channel_id=1, source_target_pairs={{0,4},{4,8},{8,12},{1,5},{5,9},{9,13},{2,6},{6,10},{10,14},{3,7},{... | collective-permute-start | bytes 147464 | tf_op jit(solution)/shard_map/ppermute | solution.py:16
  14.1 1.3 %collective-permute-start.1 = (bf16[1,2,1,4,3072]{4,2,1,0,3:T(2,128)(2,1)S(1)}, bf16[1,2,1,4,3072]{4,2,1,0,3:T(2,128)(2,1)S(1)}, u32[]{:S(2)}, u32[]{:S(2)}) collective-permute-start(bf16[1,2,1,4,3072]{4,2,1,0,3:T(2,128)(2,1)S(1)} %get-tuple-element.98), channel_id=1, source_target_pairs={{4,0},{8,4},{12,8},{5,1},{9,5},{13,9},{6,2},{10,6},{14,10},{7,3},{... | collective-permute-start | bytes 147464 | tf_op jit(solution)/shard_map/ppermute | solution.py:19
  16.5 13.4 %all-gather.3 = f32[4,1,1536]{2,1,0:T(1,128)S(1)} all-gather(f32[1,1,1536]{2,1,0:T(1,128)S(1)} %convolution_bitcast_fusion.1), channel_id=2, replica_groups=mesh['item'=2,'row'=4,'col'=4] {'col'}, dimensions={0}, use_global_device_ids=true | all-gather | bytes 30720 | tf_op jit(solution)/shard_map/all_gather | solution.py:81
  30.1 0.5 fusion.9
  30.6 0.6 slice_add_fusion
  31.3 0.7 slice_convert_fusion.8
  32.0 0.5 add_rsqrt_fusion.1
  33.3 3.5 %collective-permute-start.2 = (bf16[1,2,6,1,3072]{4,2,1,0,3:T(8,128)(2,1)S(1)}, bf16[1,2,6,1,3072]{4,2,1,0,3:T(8,128)(2,1)S(1)}, u32[]{:S(2)}, u32[]{:S(2)}) collective-permute-start(bf16[1,2,6,1,3072]{4,2,1,0,3:T(8,128)(2,1)S(1)} %get-tuple-element.95), channel_id=1, source_target_pairs={{0,1},{1,2},{2,3},{4,5},{5,6},{6,7},{8,9},{9,10},{10,11},{12,13},{... | collective-permute-start | bytes 221192 | tf_op jit(solution)/shard_map/ppermute | solution.py:16
  36.8 1.3 %collective-permute-start.3 = (bf16[1,2,6,1,3072]{4,2,1,0,3:T(8,128)(2,1)S(1)}, bf16[1,2,6,1,3072]{4,2,1,0,3:T(8,128)(2,1)S(1)}, u32[]{:S(2)}, u32[]{:S(2)}) collective-permute-start(bf16[1,2,6,1,3072]{4,2,1,0,3:T(8,128)(2,1)S(1)} %get-tuple-element.96), channel_id=1, source_target_pairs={{1,0},{2,1},{3,2},{5,4},{6,5},{7,6},{9,8},{10,9},{11,10},{13,12},{... | collective-permute-start | bytes 221192 | tf_op jit(solution)/shard_map/ppermute | solution.py:19
  38.1 0.5 iota_compare_fusion
  39.0 4.3 %collective-permute-done.3 = bf16[1,2,6,1,3072]{4,2,1,0,3:T(8,128)(2,1)S(1)} collective-permute-done((bf16[1,2,6,1,3072]{4,2,1,0,3:T(8,128)(2,1)S(1)}, bf16[1,2,6,1,3072]{4,2,1,0,3:T(8,128)(2,1)S(1)}, u32[]{:S(2)}, u32[]{:S(2)}) %collective-permute-start.3) | collective-permute-done | bytes 73760 | tf_op jit(solution)/shard_map/ppermute | solution.py:19
  43.4 0.6 maximum_maximum_fusion
  43.9 2.0 %convert_reduce_fusion.1 = (f32[2,4,4]{1,0,2:T(2,128)S(1)}, bf16[1,2,4,4,3072]{4,2,1,0,3:T(4,128)(2,1)S(1)}) fusion(f32[3072]{0:T(1024)} %bitcast.105, bf16[1,2,6,5,3072]{4,2,1,0,3:T(8,128)(2,1)S(1)} %get-tuple-element.94, f32[3072]{0:T(1024)} %bitcast.106, bf16[1,2,1,4,3072]{4,2,1,0,3:T(2,128)(2,1)S(1)} %collective-permute-done.1, ...), kind=kLoop, calls=%fused_computation.41 | loop fusion | flops 3538912 | bytes 1781888 | tf_op jit(solution)/shard_map/reduce_sum | solution.py:33
  46.5 16.8 %all_gather.17 = bf16[1,2,4,16,3072]{4,2,1,0,3:T(4,128)(2,1)S(1)} all-gather(bf16[1,2,4,4,3072]{4,2,1,0,3:T(4,128)(2,1)S(1)} %fusion.35), channel_id=1, replica_groups=mesh['item'=2,'row'=4,'col'=4] {'col'}, dimensions={3}, use_global_device_ids=true | all-gather | bytes 983040 | tf_op jit(solution)/shard_map/all_gather | solution.py:84
  63.3 1.3 %copy.31 = bf16[1,2,4,16,3072]{4,3,2,1,0:T(8,128)(2,1)} copy(bf16[1,2,4,16,3072]{4,2,1,0,3:T(4,128)(2,1)S(1)} %all_gather.17) | data formatting | bytes 1572864 | tf_op jit(solution)/shard_map/all_gather | solution.py:84
  64.6 6.2 %all-gather.6.cloned.1.call-done = bf16[3072,3,512]{2,0,1:T(8,128)(2,1)} async-done(((bf16[384,3,512]{2,0,1:T(8,128)(2,1)}), bf16[3072,3,512]{2,0,1:T(8,128)(2,1)}) %all-gather.6.cloned.1.call-update) | async-done | bytes 9437200 | tf_op jit(solution)/shard_map/all_gather | solution.py:92
  70.8 5.4 %convolution_convert_fusion = bf16[128,3,512]{2,0,1:T(8,128)(2,1)S(1)} fusion(bf16[128,3072,1]{1,0,2:T(8,128)(2,1)} %bitcast.92, bf16[3072,3,512]{2,0,1:T(8,128)(2,1)} %all-gather.6.cloned.1.call-done), kind=kOutput, calls=%fused_computation.32 | convolution fusion | flops 1208156160 | bytes 10616832 | tf_op jit(solution)/shard_map/rd,dkc->rkc/dot_general | solution.py:93
  76.2 0.7 fusion.52
  77.0 6.1 %fusion.20 = bf16[226,3,512]{2,0,1:T(8,128)(2,1)S(1)} fusion(bf16[3072,3,512]{2,0,1:T(8,128)(2,1)} %all-gather.6.cloned.1.call-done, bf16[1,226,3072]{2,1,0:T(8,128)(2,1)S(1)} %copy-done.1, f32[3072]{0:T(1024)S(1)} %bitcast.110, f32[3072]{0:T(1024)S(1)} %bitcast.108, f32[226]{0:T(256)S(1)} %copy-done.8, f32[226]{0:T(256)S(1)} %broadcast_multiply_fusion.1), kind=kOutput, calls=%fused_computation.28 | convolution fusion | flops 2137316352 | bytes 11546384 | tf_op jit(solution)/shard_map/rd,dkc->rkc/dot_general | solution.py:96
  83.2 0.7 fusion.51
  84.7 1.1 copy.33
  85.8 10.8 %all-gather.1 = bf16[512,1,512]{2,0,1:T(8,128)(2,1)} all-gather(bf16[128,1,512]{2,0,1:T(8,128)(2,1)S(1)} %copy-done.2), channel_id=3, replica_groups=mesh['item'=2,'row'=4,'col'=4] {'row'}, dimensions={0}, use_global_device_ids=true | all-gather | bytes 655360 | tf_op jit(solution)/shard_map/all_gather | solution.py:112
  96.6 10.4 %all-gather.2 = bf16[512,1,512]{2,0,1:T(8,128)(2,1)} all-gather(bf16[128,1,512]{2,0,1:T(8,128)(2,1)S(1)} %get-tuple-element.90), channel_id=4, replica_groups=mesh['item'=2,'row'=4,'col'=4] {'row'}, dimensions={0}, use_global_device_ids=true | all-gather | bytes 655360 | tf_op jit(solution)/shard_map/all_gather | solution.py:113
  107.3 7.7 %while.14 = (s32[]{:T(128)}, f32[128,8]{0,1:T(8,128)S(1)}, f32[128,8]{0,1:T(8,128)S(1)}, f32[128,8,64]{0,2,1:T(8,128)S(1)}, bf16[4,128,512]{2,1,0:T(8,128)(2,1)}...) while((s32[]{:T(128)}, f32[128,8]{0,1:T(8,128)S(1)}, ...), condition=%wide.region_9.10_spmd, body=%wide.region_6.9_spmd.sunk | while | flops 34473984 | bytes 3604569 | solution.py:120
  107.3 1.0 constant_dynamic-slice_fusion.3
  109.3 1.0 constant_dynamic-slice_fusion.3
  111.2 1.0 constant_dynamic-slice_fusion.3
  113.1 1.0 constant_dynamic-slice_fusion.3
  115.3 0.9 reshape.176
  (75 shorter events, 6.6 us)
Async XLA Ops:
  6.5 9.6 %copy-start = (bf16[512,1536]{1,0:T(8,128)(2,1)S(1)}, bf16[512,1536]{1,0:T(8,128)(2,1)}, u32[]{:S(2)}) copy-start(bf16[512,1536]{1,0:T(8,128)(2,1)} %param.12) | copy-start | bytes 4718596
  6.5 23.3 %copy-start.1 = (bf16[1,226,3072]{2,1,0:T(8,128)(2,1)S(1)}, bf16[1,226,3072]{2,1,0:T(8,128)(2,1)}, u32[]{:S(2)}) copy-start(bf16[1,226,3072]{2,1,0:T(8,128)(2,1)} %param.10) | copy-start | bytes 4165636
  6.5 64.3 %all-gather.6.cloned.1.call-start = ((), (), s32[]{:S(2)}) async-start(), calls=%async_computation | async-start | bytes 10616832 | tf_op jit(solution)/shard_map/all_gather | solution.py:92
  7.3 24.0 %copy-start.3 = (bf16[3,3,3072]{2,1,0:T(4,128)(2,1)S(1)}, bf16[3,3,3072]{2,1,0:T(4,128)(2,1)}, u32[]{:S(2)}) copy-start(bf16[3,3,3072]{2,1,0:T(4,128)(2,1)} %param.11) | copy-start | bytes 165892
  9.3 23.9 %collective-permute-start = (bf16[1,2,1,4,3072]{4,2,1,0,3:T(2,128)(2,1)}, bf16[1,2,1,4,3072]{4,2,1,0,3:T(2,128)(2,1)S(1)}, u32[]{:S(2)}, u32[]{:S(2)}) collective-permute-start(bf16[1,2,1,4,3072]{4,2,1,0,3:T(2,128)(2,1)} %get-tuple-element.97), channel_id=1, source_target_pairs={{0,4},{4,8},{8,12},{1,5},{5,9},{9,13},{2,6},{6,10},{10,14},{3,7},{... | collective-permute-start | bytes 147464 | tf_op jit(solution)/shard_map/ppermute | solution.py:16
  14.1 19.1 %collective-permute-start.1 = (bf16[1,2,1,4,3072]{4,2,1,0,3:T(2,128)(2,1)S(1)}, bf16[1,2,1,4,3072]{4,2,1,0,3:T(2,128)(2,1)S(1)}, u32[]{:S(2)}, u32[]{:S(2)}) collective-permute-start(bf16[1,2,1,4,3072]{4,2,1,0,3:T(2,128)(2,1)S(1)} %get-tuple-element.98), channel_id=1, source_target_pairs={{4,0},{8,4},{12,8},{5,1},{9,5},{13,9},{6,2},{10,6},{14,10},{7,3},{... | collective-permute-start | bytes 147464 | tf_op jit(solution)/shard_map/ppermute | solution.py:19
  33.1 13.1 %copy-start.4 = (f32[1,3072]{1,0:T(1,128)S(1)}, f32[1,3072]{1,0:T(1,128)}, u32[]{:S(2)}) copy-start(f32[1,3072]{1,0:T(1,128)} %get-tuple-element.108) | copy-start | bytes 36868
  33.1 13.1 %copy-start.6 = (f32[1,3072]{1,0:T(1,128)S(1)}, f32[1,3072]{1,0:T(1,128)}, u32[]{:S(2)}) copy-start(f32[1,3072]{1,0:T(1,128)} %get-tuple-element.109) | copy-start | bytes 36868
  33.3 5.7 %collective-permute-start.2 = (bf16[1,2,6,1,3072]{4,2,1,0,3:T(8,128)(2,1)S(1)}, bf16[1,2,6,1,3072]{4,2,1,0,3:T(8,128)(2,1)S(1)}, u32[]{:S(2)}, u32[]{:S(2)}) collective-permute-start(bf16[1,2,6,1,3072]{4,2,1,0,3:T(8,128)(2,1)S(1)} %get-tuple-element.95), channel_id=1, source_target_pairs={{0,1},{1,2},{2,3},{4,5},{5,6},{6,7},{8,9},{9,10},{10,11},{12,13},{... | collective-permute-start | bytes 221192 | tf_op jit(solution)/shard_map/ppermute | solution.py:16
  36.8 6.5 %collective-permute-start.3 = (bf16[1,2,6,1,3072]{4,2,1,0,3:T(8,128)(2,1)S(1)}, bf16[1,2,6,1,3072]{4,2,1,0,3:T(8,128)(2,1)S(1)}, u32[]{:S(2)}, u32[]{:S(2)}) collective-permute-start(bf16[1,2,6,1,3072]{4,2,1,0,3:T(8,128)(2,1)S(1)} %get-tuple-element.96), channel_id=1, source_target_pairs={{1,0},{2,1},{3,2},{5,4},{6,5},{7,6},{9,8},{10,9},{11,10},{13,12},{... | collective-permute-start | bytes 221192 | tf_op jit(solution)/shard_map/ppermute | solution.py:19
  70.8 6.2 %copy-start.5 = (f32[1,3072]{1,0:T(1,128)S(1)}, f32[1,3072]{1,0:T(1,128)}, u32[]{:S(2)}) copy-start(f32[1,3072]{1,0:T(1,128)} %get-tuple-element.108) | copy-start | bytes 36868
  70.8 6.2 %copy-start.7 = (f32[1,3072]{1,0:T(1,128)S(1)}, f32[1,3072]{1,0:T(1,128)}, u32[]{:S(2)}) copy-start(f32[1,3072]{1,0:T(1,128)} %get-tuple-element.109) | copy-start | bytes 36868
  70.8 6.2 %copy-start.8 = (f32[226]{0:T(256)S(1)}, f32[226]{0:T(256)}, u32[]{:S(2)}) copy-start(f32[226]{0:T(256)} %add_rsqrt_fusion.1) | copy-start | bytes 2716
  77.0 7.0 %copy-start.9 = (pred[226]{0:T(512)(128)(4,1)S(1)}, pred[226]{0:T(512)(128)(4,1)}, u32[]{:S(2)}) copy-start(pred[226]{0:T(512)(128)(4,1)} %iota_compare_fusion) | copy-start | bytes 682
  83.2 2.6 %copy-start.2 = (bf16[128,1,512]{2,0,1:T(8,128)(2,1)S(1)}, bf16[128,1,512]{2,0,1:T(8,128)(2,1)}, u32[]{:S(2)}) copy-start(bf16[128,1,512]{2,0,1:T(8,128)(2,1)} %get-tuple-element.91) | copy-start | bytes 393220
Sparse Core Ops, SparseCore 0:
  9.3 61.5 all-gather.5
where the time goes:
time: 123 us
  blocking collectives  51.4 us (42%)
  between operations  15 us (12%)
  matrix products  14.7 us (12%)
  local copies, waits for them, and re-layouts  12 us (10%)
  waiting for transfers between devices  11.6 us (9%)
  starting transfers between devices  10.9 us (9%)
  other arithmetic  7.13 us (6%)
    all_gather x1, blocking collectives, on_device(): lax.all_gather(modulate(convolved, shift, scale), 'col', axis=3, tiled=True)  16.8 us
    all_gather x1, blocking collectives, on_device(): modulation = lax.all_gather(own_columns, 'col', axis=1, tiled=True)[0]  13.4 us
    all_gather x1, blocking collectives, on_device(): key_rows = lax.all_gather(local_keys, 'row', axis=0, tiled=True)  10.8 us
    all_gather x1, blocking collectives, on_device(): value_rows = lax.all_gather(local_values, 'row', axis=0, tiled=True)  10.4 us
    ppermute x2, starting transfers between devices, with_halo(): lax.ppermute(lax.slice_in_dim(block, block.shape[dim] - width, None, axis...  8.32 us
    all_gather x1, waiting for transfers between devices, on_device(): lax.all_gather(qkv_weight, ('item', 'row'), axis=0, tiled=True)  6.19 us
    dot_general x1, matrix products, on_device(): jnp.einsum('rd,dkc->rkc', text_normed, full_weight, preferred_element_typ...  6.14 us
    dot_general x1, matrix products, on_device(): jnp.einsum('rd,dkc->rkc', flat_rows, full_weight, preferred_element_type=...  5.36 us
  transfers between devices with their start and end apart: 5, of which 3 were waited for; matrix products, arithmetic and copies ran while one was open for 8% of the time, Pallas kernels for 0%

commit v1 on v0

--- a/solution.py
+++ b/solution.py
@@ -1,11 +1,16 @@
+import functools
 import math
 
 import jax
 import jax.numpy as jnp
 from jax import lax
+from jax.experimental import pallas as pl
+from jax.experimental.pallas import tpu as pltpu
 from jax.sharding import PartitionSpec as P
 
 HD = 64
+MESH = pl.DeviceIdType.MESH
+VMEM = pltpu.VMEM
 
 
 def with_halo(block, sides, width):
@@ -60,7 +65,7 @@
     return (newest, running_sum, weighted)
 
 
-def on_device(latents, prompt_rows, peg_weight, modulation_weight, qkv_weight, text_len, timestep):
+def on_device_general(latents, prompt_rows, peg_weight, modulation_weight, qkv_weight, text_len, timestep):
     tile_h = latents.shape[2]
     tile_w = latents.shape[3]
     width = latents.shape[4]
@@ -130,6 +135,385 @@
     return attended.reshape(1, frames, tile_h, grid_w, head_width)
 
 
+def centered_rows(values):
+    center = jnp.mean(values, axis=-1, keepdims=True)
+    centered = values - center
+    spread = jnp.mean(centered * centered, axis=-1, keepdims=True)
+    return centered * lax.rsqrt(spread + 1e-06)
+
+
+def layer_kernel(
+    sizes,
+    len_ref,
+    tile_ref,
+    prompt_ref,
+    act_ref,
+    mod_ref,
+    weight_ref,
+    out_ref,
+    mod_buf,
+    affine,
+    weights,
+    text_in,
+    send_x,
+    grid_x,
+    send_text,
+    recv_text,
+    own_text,
+    send_part,
+    recv_part,
+    own_part,
+    q_buf,
+    k_buf,
+    v_buf,
+    send_out,
+    recv_out,
+    w_sems,
+    mod_send,
+    mod_recv,
+    x_send,
+    x_recv,
+    z_send,
+    z_recv,
+    t_send,
+    t_recv,
+    p_send,
+    p_recv,
+    o_send,
+    o_recv,
+):
+    rows, cols, text, padded_text, tile_w = sizes
+    tokens, width = tile_ref.shape
+    depth = weight_ref.shape[1]
+    out_w = weight_ref.shape[2] // 3
+    block = tokens * cols
+    item = lax.axis_index("item")
+    row = lax.axis_index("row")
+    col = lax.axis_index("col")
+
+    def row_peer(step):
+        return lax.rem(row + step, rows)
+
+    def col_peer(step):
+        return lax.rem(col + step, cols)
+
+    def remote(src, dst, send, recv, where):
+        return pltpu.make_async_remote_copy(
+            src_ref=src, dst_ref=dst, send_sem=send, recv_sem=recv, device_id=where, device_id_type=MESH
+        )
+
+    barrier = pltpu.get_barrier_semaphore()
+    pl.semaphore_signal(barrier, inc=1, device_id={"item": 1 - item}, device_id_type=MESH)
+    for step in range(1, rows):
+        pl.semaphore_signal(barrier, inc=1, device_id={"row": row_peer(step)}, device_id_type=MESH)
+    for step in range(1, cols):
+        pl.semaphore_signal(barrier, inc=1, device_id={"col": col_peer(step)}, device_id_type=MESH)
+
+    own_columns = jnp.dot(act_ref[...], mod_ref[...], preferred_element_type=jnp.float32)
+    mod_buf[col] = own_columns[0:1, :]
+    pl.semaphore_wait(barrier, rows + cols - 1)
+    mod_copies = []
+    for step in range(1, cols):
+        copy = remote(
+            mod_buf.at[col],
+            mod_buf.at[col],
+            mod_send.at[step - 1],
+            mod_recv.at[step - 1],
+            {"col": col_peer(step)},
+        )
+        copy.start()
+        mod_copies.append(copy)
+    weight_copy = remote(
+        weight_ref,
+        weights.at[:, pl.ds(depth, depth), :],
+        w_sems.at[0],
+        w_sems.at[1],
+        {"item": 1 - item},
+    )
+    weight_copy.start()
+    for dest in range(rows):
+        weights[dest, 0:depth, :] = weight_ref[dest]
+    tile_normal = centered_rows(tile_ref[...].astype(jnp.float32))
+    for step in range(1, cols):
+        remote(
+            mod_buf.at[col],
+            mod_buf.at[lax.rem(col - step + cols, cols)],
+            mod_send.at[step - 1],
+            mod_recv.at[step - 1],
+            {"col": col_peer(step)},
+        ).wait_recv()
+    half = cols // 2
+    piece = mod_buf.shape[2]
+    for part in range(half):
+        affine[0, :, part * piece : (part + 1) * piece] = mod_buf[part]
+        affine[1, :, part * piece : (part + 1) * piece] = 1.0 + mod_buf[half + part]
+
+    def depth_slices(dest):
+        first = (item * rows + dest) * depth
+        second = ((1 - item) * rows + dest) * depth
+        return (pl.multiple_of(first, depth), pl.multiple_of(second, depth))
+
+    text_in[0:tokens, :] = (tile_normal * affine[1] + affine[0]).astype(jnp.bfloat16)
+    x_copies = []
+    for step in range(1, rows):
+        peer = row_peer(step)
+        for order, start in enumerate(depth_slices(peer)):
+            send_x[step - 1, :, order * depth : (order + 1) * depth] = text_in[
+                0:tokens, pl.ds(start, depth)
+            ]
+        copy = remote(
+            send_x.at[step - 1],
+            grid_x.at[0, pl.ds(pl.multiple_of(row * tokens, tokens), tokens), :],
+            x_send.at[step - 1],
+            x_recv.at[step - 1],
+            {"row": peer},
+        )
+        copy.start()
+        x_copies.append(copy)
+    own_slices = depth_slices(row)
+    for order, start in enumerate(own_slices):
+        grid_x[
+            0, pl.ds(pl.multiple_of(row * tokens, tokens), tokens), order * depth : (order + 1) * depth
+        ] = text_in[0:tokens, pl.ds(start, depth)]
+
+    for step in range(1, rows):
+        source = lax.rem(row - step + rows, rows)
+        remote(
+            send_x.at[step - 1],
+            grid_x.at[0, pl.ds(pl.multiple_of(source * tokens, tokens), tokens), :],
+            x_send.at[step - 1],
+            x_recv.at[step - 1],
+            {"row": row_peer(step)},
+        ).wait_recv()
+    z_copies = []
+    for step in range(1, cols):
+        copy = remote(
+            grid_x.at[0], grid_x.at[step], z_send.at[step - 1], z_recv.at[step - 1], {"col": col_peer(step)}
+        )
+        copy.start()
+        z_copies.append(copy)
+    weight_copy.wait_recv()
+
+    p_copies = []
+
+    def latent_part(group):
+        values = grid_x[group]
+        for step in range(1, rows):
+            peer = row_peer(step)
+            send_part[group, step - 1] = jnp.dot(
+                values, weights[peer], preferred_element_type=jnp.float32
+            ).astype(jnp.bfloat16)
+            copy = remote(
+                send_part.at[group, step - 1],
+                recv_part.at[group, step - 1],
+                p_send.at[group, step - 1],
+                p_recv.at[group, step - 1],
+                {"row": peer},
+            )
+            copy.start()
+            p_copies.append(copy)
+        own_part[group] = jnp.dot(values, weights[row], preferred_element_type=jnp.float32)
+
+    latent_part(0)
+
+    scale_pieces = [affine[1, :, pl.ds(start, depth)] for start in own_slices]
+    shift_pieces = [affine[0, :, pl.ds(start, depth)] for start in own_slices]
+    for start_row in range(0, padded_text, 16):
+        count = min(16, text - start_row)
+        values = prompt_ref[start_row : start_row + count, :].astype(jnp.float32)
+        center = jnp.mean(values, axis=-1, keepdims=True)
+        centered = values - center
+        spread = lax.rsqrt(jnp.mean(centered * centered, axis=-1, keepdims=True) + 1e-06)
+        for order, start in enumerate(own_slices):
+            part = prompt_ref[start_row : start_row + count, pl.ds(start, depth)].astype(jnp.float32)
+            normed = (part - center) * spread * scale_pieces[order] + shift_pieces[order]
+            if count < 16:
+                normed = jnp.concatenate([normed, jnp.zeros((16 - count, depth), jnp.float32)], axis=0)
+            text_in[start_row : start_row + 16, order * depth : (order + 1) * depth] = normed.astype(
+                jnp.bfloat16
+            )
+    text_values = text_in[:, 0 : 2 * depth]
+    t_copies = []
+    for step in range(1, rows):
+        peer = row_peer(step)
+        send_text[step - 1] = jnp.dot(
+            text_values, weights[peer, :, out_w:], preferred_element_type=jnp.float32
+        ).astype(jnp.bfloat16)
+        copy = remote(
+            send_text.at[step - 1],
+            recv_text.at[step - 1],
+            t_send.at[step - 1],
+            t_recv.at[step - 1],
+            {"row": peer},
+        )
+        copy.start()
+        t_copies.append(copy)
+    own_text[...] = jnp.dot(text_values, weights[row, :, out_w:], preferred_element_type=jnp.float32)
+
+    for group in range(1, cols):
+        z_copies[group - 1].wait_recv()
+        latent_part(group)
+
+    for copy in t_copies:
+        copy.wait_recv()
+    total = own_text[...]
+    for step in range(1, rows):
+        total = total + recv_text[step - 1].astype(jnp.float32)
+    k_buf[0:padded_text, :] = total[:, 0:out_w].astype(jnp.bfloat16)
+    v_buf[0:padded_text, :] = total[:, out_w:].astype(jnp.bfloat16)
+    for group in range(cols):
+        for step in range(1, rows):
+            p_copies[group * (rows - 1) + step - 1].wait_recv()
+        total = own_part[group]
+        for step in range(1, rows):
+            total = total + recv_part[group, step - 1].astype(jnp.float32)
+        rounded = total.astype(jnp.bfloat16)
+        per_col = rows * tokens
+        base = padded_text + group * per_col
+        k_buf[base : base + per_col, :] = rounded[:, out_w : 2 * out_w]
+        v_buf[base : base + per_col, :] = rounded[:, 2 * out_w :]
+        for dest in range(rows):
+            q_buf[dest, group * tokens : (group + 1) * tokens, :] = rounded[
+                dest * tokens : (dest + 1) * tokens, 0:out_w
+            ]
+
+    at = lax.broadcasted_iota(jnp.int32, (block, block), 0)
+    source = lax.broadcasted_iota(jnp.int32, (block, block), 1)
+    group = source // tokens
+    token = source - group * tokens
+    line = token // tile_w
+    place = token - line * tile_w
+    owner = col - group
+    owner = jnp.where(owner < 0, owner + cols, owner)
+    target = (line * cols + owner) * tile_w + place
+    permute = jnp.where(at == target, 1.0, 0.0).astype(jnp.bfloat16)
+    keys = k_buf[...]
+    vals = v_buf[...]
+    position = lax.broadcasted_iota(jnp.int32, (1, keys.shape[0]), 1)
+    valid = (position >= padded_text) | (position < len_ref[0])
+    o_copies = []
+    for step in list(range(1, rows)) + [0]:
+        peer = row_peer(step)
+        queries = jnp.dot(permute, q_buf[peer], preferred_element_type=jnp.float32).astype(jnp.bfloat16)
+        outs = []
+        for head in range(out_w // HD):
+            lanes = slice(head * HD, (head + 1) * HD)
+            scores = (
+                lax.dot_general(
+                    queries[:, lanes],
+                    keys[:, lanes],
+                    (((1,), (1,)), ((), ())),
+                    preferred_element_type=jnp.float32,
+                )
+                * 0.125
+            )
+            scores = jnp.where(valid, scores, -jnp.inf)
+            weight = jnp.exp(scores - jnp.max(scores, axis=-1, keepdims=True))
+            total = jnp.sum(weight, axis=-1, keepdims=True)
+            outs.append(
+                jnp.dot(weight.astype(jnp.bfloat16), vals[:, lanes], preferred_element_type=jnp.float32)
+                / total
+            )
+        result = jnp.concatenate(outs, axis=-1).astype(jnp.bfloat16)
+        if step == 0:
+            recv_out[row] = result
+        else:
+            send_out[step - 1] = result
+            copy = remote(
+                send_out.at[step - 1],
+                recv_out.at[row],
+                o_send.at[step - 1],
+                o_recv.at[step - 1],
+                {"row": peer},
+            )
+            copy.start()
+            o_copies.append(copy)
+    for step in range(1, rows):
+        source = lax.rem(row - step + rows, rows)
+        remote(
+            send_out.at[step - 1],
+            recv_out.at[source],
+            o_send.at[step - 1],
+            o_recv.at[step - 1],
+            {"row": row_peer(step)},
+        ).wait_recv()
+    for source in range(rows):
+        out_ref[:, source * out_w : (source + 1) * out_w] = recv_out[source]
+    for copy in mod_copies + [weight_copy] + x_copies + z_copies + p_copies + t_copies + o_copies:
+        copy.wait_send()
+
+
+def on_device_fast(
+    rows, cols, latents, prompt_rows, peg_weight, modulation_weight, qkv_weight, text_len, timestep
+):
+    frames, tile_h, tile_w, width = latents.shape[1:]
+    padded = with_halo(latents, (("row", 2), ("col", 3)), 1)
+    summed = latents.astype(jnp.float32)
+    for row_tap in range(3):
+        for col_tap in range(3):
+            summed = summed + padded[
+                :, :, row_tap : row_tap + tile_h, col_tap : col_tap + tile_w, :
+            ].astype(jnp.float32) * peg_weight[row_tap, col_tap].astype(jnp.float32)
+    tokens = frames * tile_h * tile_w
+    tile = summed.astype(jnp.bfloat16).reshape(tokens, width)
+    temb = modulation_weight.shape[0]
+    activation = jax.nn.silu(time_angles(timestep[0], temb)).astype(jnp.bfloat16)
+    activation = jnp.broadcast_to(activation[None, :], (16, temb))
+    depth, parts, head_width = qkv_weight.shape
+    out_w = head_width // rows
+    by_dest = qkv_weight.reshape(depth, parts, rows, out_w).transpose(2, 0, 1, 3)
+    by_dest = by_dest.reshape(rows, depth, parts * out_w)
+    text = prompt_rows.shape[1]
+    padded_text = -(-text // 16) * 16
+    block = tokens * cols
+    group_rows = tokens * rows
+    bf16, f32 = jnp.bfloat16, jnp.float32
+    dma = pltpu.SemaphoreType.DMA
+    all_rows = padded_text + group_rows * cols
+    attended = pl.pallas_call(
+        functools.partial(layer_kernel, (rows, cols, text, padded_text, tile_w)),
+        out_shape=jax.ShapeDtypeStruct((block, head_width), bf16),
+        in_specs=[pl.BlockSpec(memory_space=pltpu.SMEM)] + [pl.BlockSpec(memory_space=VMEM)] * 5,
+        out_specs=pl.BlockSpec(memory_space=VMEM),
+        scratch_shapes=[
+            VMEM((cols, 1, modulation_weight.shape[1]), f32),
+            VMEM((2, 1, width), f32),
+            VMEM((rows, 2 * depth, parts * out_w), bf16),
+            VMEM((max(padded_text, tokens), width), bf16),
+            VMEM((rows - 1, tokens, 2 * depth), bf16),
+            VMEM((cols, group_rows, 2 * depth), bf16),
+            VMEM((rows - 1, padded_text, 2 * out_w), bf16),
+            VMEM((rows - 1, padded_text, 2 * out_w), bf16),
+            VMEM((padded_text, 2 * out_w), f32),
+            VMEM((cols, rows - 1, group_rows, parts * out_w), bf16),
+            VMEM((cols, rows - 1, group_rows, parts * out_w), bf16),
+            VMEM((cols, group_rows, parts * out_w), f32),
+            VMEM((rows, block, out_w), bf16),
+            VMEM((all_rows, out_w), bf16),
+            VMEM((all_rows, out_w), bf16),
+            VMEM((rows - 1, block, out_w), bf16),
+            VMEM((rows, block, out_w), bf16),
+            dma((2,)),
+            dma((cols - 1,)),
+            dma((cols - 1,)),
+            dma((rows - 1,)),
+            dma((rows - 1,)),
+            dma((cols - 1,)),
+            dma((cols - 1,)),
+            dma((rows - 1,)),
+            dma((rows - 1,)),
+            dma((cols, rows - 1)),
+            dma((cols, rows - 1)),
+            dma((rows - 1,)),
+            dma((rows - 1,)),
+        ],
+        compiler_params=pltpu.CompilerParams(
+            collective_id=0, has_side_effects=True, vmem_limit_bytes=48 * 1024 * 1024
+        ),
+    )(text_len, tile, prompt_rows[0], activation, modulation_weight, by_dest)
+    return attended.reshape(1, frames, tile_h, tile_w * cols, head_width)
+
+
 def solution(mesh):
     in_specs = (
         P("item", None, "row", "col", None),
@@ -141,6 +525,14 @@
         P("item"),
     )
     out_specs = P("item", None, "row", None, "col")
+    rows, cols, items = mesh.shape["row"], mesh.shape["col"], mesh.shape["item"]
+
+    def on_device(*blocks):
+        group = blocks[4].shape[2] // rows
+        if items == 2 and cols % 2 == 0 and group >= 128 and group % 128 == 0:
+            return on_device_fast(rows, cols, *blocks)
+        return on_device_general(*blocks)
+
     return jax.shard_map(
         on_device, mesh=mesh, in_specs=in_specs, out_specs=out_specs, check_vma=False
     )

time: 123 us -> 68.4 us (0.56)
  blocking collectives: 51.4 us -> 0 us
  Pallas kernels: 0 us -> 41.3 us
  matrix products: 14.7 us -> 0 us
  between operations: 15 us -> 1.47 us
  local copies, waits for them, and re-layouts: 12 us -> 5.89 us
  waiting for transfers between devices: 11.6 us -> 5.72 us
  other arithmetic: 7.13 us -> 2.56 us
    all_gather x4 -> x0, blocking collectives: 51.4 us -> none  [the longest x1 16.8 us: on_device(): lax.all_gather(modulate(convolved, shift, scale), 'col', axis=3, tiled=True)]
    pallas_call x0 -> x1, Pallas kernels: none -> 41.3 us  [on_device_fast(): pl.pallas_call(functools.partial(layer_kernel, (rows, cols, text, padded_...]
    dot_general x13 -> x0, matrix products: 14.7 us -> none  [the longest x1 6.14 us: on_device(): jnp.einsum('rd,dkc->rkc', text_normed, full_weight, preferred_element_typ...]
    all_gather x1 -> x0, waiting for transfers between devices: 6.19 us -> none  [on_device(): lax.all_gather(qkv_weight, ('item', 'row'), axis=0, tiled=True)]
    dynamic_slice x12 -> x0, local copies, waits for them, and re-layouts: 4.9 us -> none  [on_device(): lax.scan(one_block, text_carry, (key_rows.reshape(block_count, row_count,...]
    reduce_sum x9 -> x0, other arithmetic: 3.61 us -> none  [the longest x2 2.31 us: modulate(): center = jnp.mean(values, axis=-1, keepdims=True)]
    unnamed x21 -> x10, local copies, waits for them, and re-layouts: 1.25 us -> 3.83 us
    slice x5 -> x1, local copies, waits for them, and re-layouts: 2.73 us -> 0.86 us  [with_halo(): lax.slice_in_dim(block, 0, width, axis=dim)]
  transfers between devices with their start and end apart: 5 -> 4, of which waited for: 3 -> 2; matrix products, arithmetic and copies ran while one was open for 8% -> 6% of each run, Pallas kernels for 0% -> 0%
where the time goes in v1:
time: 68.4 us; the launch traced here: 68 us
  Pallas kernels  41.3 us (60%)
  starting transfers between devices  11 us (16%)
  local copies, waits for them, and re-layouts  5.89 us (9%)
  waiting for transfers between devices  5.72 us (8%)
  other arithmetic  2.56 us (4%)
  between operations  1.47 us (2%)
    pallas_call x1, Pallas kernels, on_device_fast(): pl.pallas_call(functools.partial(layer_kernel, (rows, cols, text, padded_...  41.3 us
    ppermute x2, starting transfers between devices, with_halo(): lax.ppermute(lax.slice_in_dim(block, block.shape[dim] - width, None, axis...  8.47 us
    ppermute x2, waiting for transfers between devices, with_halo(): lax.ppermute(lax.slice_in_dim(block, 0, width, axis=dim), axis, backward)  4.24 us
    unnamed x10, local copies, waits for them, and re-layouts  3.83 us
    ppermute x2, starting transfers between devices, with_halo(): lax.ppermute(lax.slice_in_dim(block, 0, width, axis=dim), axis, backward)  2.58 us
    ppermute x2, waiting for transfers between devices, with_halo(): lax.ppermute(lax.slice_in_dim(block, block.shape[dim] - width, None, axis...  1.48 us
    convert_element_type x1, other arithmetic, on_device_fast(): tile = summed.astype(jnp.bfloat16).reshape(tokens, width)  1.44 us
  transfers between devices with their start and end apart: 4, of which 2 were waited for; matrix products, arithmetic and copies ran while one was open for 6% of the time, Pallas kernels for 0%

profile of v1, /device:TPU:0, one launch (start us, length us, event | category | flops | bytes accessed | tf_op | source)
XLA Modules:
  0.0 68.0 jit_solution(4287376590936371932)
XLA Ops:
  0.0 0.9 %fusion.17 = (bf16[1,2,1,4,3072]{4,3,2,1,0:T(4,128)(2,1)S(1)}, bf16[1,2,1,4,3072]{4,3,2,1,0:T(4,128)(2,1)S(1)}) fusion(bf16[1,2,4,4,3072]{4,3,2,1,0:T(4,128)(2,1)} %param.7), kind=kLoop, calls=%fused_computation.46 | loop fusion | bytes 196608 | tf_op jit(solution)/shard_map/slice | solution.py:24
  0.9 4.8 %collective-permute-start = (bf16[1,2,1,4,3072]{4,3,2,1,0:T(4,128)(2,1)S(1)}, bf16[1,2,1,4,3072]{4,3,2,1,0:T(4,128)(2,1)S(1)}, u32[]{:S(2)}, u32[]{:S(2)}) collective-permute-start(bf16[1,2,1,4,3072]{4,3,2,1,0:T(4,128)(2,1)S(1)} %get-tuple-element.8), channel_id=1, source_target_pairs={{0,4},{4,8},{8,12},{1,5},{5,9},{9,13},{2,6},{6,10},{10,14},{3,7},{... | collective-permute-start | bytes 147464 | tf_op jit(solution)/shard_map/ppermute | solution.py:21
  5.7 1.3 %collective-permute-start.1 = (bf16[1,2,1,4,3072]{4,3,2,1,0:T(4,128)(2,1)S(1)}, bf16[1,2,1,4,3072]{4,3,2,1,0:T(4,128)(2,1)S(1)}, u32[]{:S(2)}, u32[]{:S(2)}) collective-permute-start(bf16[1,2,1,4,3072]{4,3,2,1,0:T(4,128)(2,1)S(1)} %get-tuple-element.7), channel_id=1, source_target_pairs={{4,0},{8,4},{12,8},{5,1},{9,5},{13,9},{6,2},{10,6},{14,10},{7,3},{... | collective-permute-start | bytes 147464 | tf_op jit(solution)/shard_map/ppermute | solution.py:24
  7.0 1.1 %slice_convert_fusion.8 = (f32[1,1,3072]{2,1,0:T(1,128)S(1)}, f32[1,1,3072]{2,1,0:T(1,128)S(1)}, f32[1,1,3072]{2,1,0:T(1,128)S(1)}, f32[1,1,3072]{2,1,0:T(1,128)...) fusion(bf16[3,3,3072]{2,1,0:T(4,128)(2,1)} %param.9), kind=kLoop, calls=%fused_computation.35 | loop fusion | flops 27648 | bytes 165888 | tf_op jit(solution)/shard_map/convert_element_type | solution.py:456
  8.8 1.7 %copy.10 = bf16[384,3,512]{0,2,1:T(8,128)(2,1)S(1)} copy(bf16[384,3,512]{2,0,1:T(8,128)(2,1)} %param.11) | data formatting | bytes 2359296 | tf_op args[4]
  10.5 0.1 copy.11
  10.6 0.0 copy-start.2
  10.6 0.8 %copy.12.weight_ref = bf16[4,384,384]{2,1,0:T(8,128)(2,1)S(1)} copy(bf16[4,384,384]{1,2,0:T(8,128)(2,1)S(1)} %bitcast.18) | data formatting | bytes 2359296 | tf_op jit(solution)/shard_map/reshape | solution.py:465
  12.1 0.0 collective-permute-done
  12.1 0.0 copy-done.2
  12.1 0.1 constant_dynamic-update-slice_fusion.1
  12.2 0.0 copy-start
  12.2 0.0 collective-permute-done.1
  12.3 0.2 fusion.16
  12.5 3.6 %collective-permute-start.2 = (bf16[1,2,6,1,3072]{4,3,2,1,0:T(2,128)(2,1)S(1)}, bf16[1,2,6,1,3072]{4,3,2,1,0:T(2,128)(2,1)S(1)}, u32[]{:S(2)}, u32[]{:S(2)}) collective-permute-start(bf16[1,2,6,1,3072]{4,3,2,1,0:T(2,128)(2,1)S(1)} %get-tuple-element.5), channel_id=1, source_target_pairs={{0,1},{1,2},{2,3},{4,5},{5,6},{6,7},{8,9},{9,10},{10,11},{12,13},{... | collective-permute-start | bytes 221192 | tf_op jit(solution)/shard_map/ppermute | solution.py:21
  16.1 1.3 %collective-permute-start.3 = (bf16[1,2,6,1,3072]{4,3,2,1,0:T(2,128)(2,1)S(1)}, bf16[1,2,6,1,3072]{4,3,2,1,0:T(2,128)(2,1)S(1)}, u32[]{:S(2)}, u32[]{:S(2)}) collective-permute-start(bf16[1,2,6,1,3072]{4,3,2,1,0:T(2,128)(2,1)S(1)} %get-tuple-element.6), channel_id=1, source_target_pairs={{1,0},{2,1},{3,2},{5,4},{6,5},{7,6},{9,8},{10,9},{11,10},{13,12},{... | collective-permute-start | bytes 221192 | tf_op jit(solution)/shard_map/ppermute | solution.py:24
  17.4 1.5 %collective-permute-done.2 = bf16[1,2,6,1,3072]{4,3,2,1,0:T(2,128)(2,1)S(1)} collective-permute-done((bf16[1,2,6,1,3072]{4,3,2,1,0:T(2,128)(2,1)S(1)}, bf16[1,2,6,1,3072]{4,3,2,1,0:T(2,128)(2,1)S(1)}, u32[]{:S(2)}, u32[]{:S(2)}) %collective-permute-start.2) | collective-permute-done | bytes 73760 | tf_op jit(solution)/shard_map/ppermute | solution.py:21
  18.9 4.2 %collective-permute-done.3 = bf16[1,2,6,1,3072]{4,3,2,1,0:T(2,128)(2,1)S(1)} collective-permute-done((bf16[1,2,6,1,3072]{4,3,2,1,0:T(2,128)(2,1)S(1)}, bf16[1,2,6,1,3072]{4,3,2,1,0:T(2,128)(2,1)S(1)}, u32[]{:S(2)}, u32[]{:S(2)}) %collective-permute-start.3) | collective-permute-done | bytes 73760 | tf_op jit(solution)/shard_map/ppermute | solution.py:24
  23.1 1.4 %fusion.8 = bf16[1,2,4,4,3072]{4,3,2,1,0:T(4,128)(2,1)S(1)} fusion(bf16[1,2,4,4,3072]{4,3,2,1,0:T(4,128)(2,1)S(1)} %copy-done.2, bf16[1,2,6,4,3072]{4,3,2,1,0:T(4,128)(2,1)S(1)} %constant_dynamic-update-slice_fusion, bf16[1,2,6,1,3072]{4,3,2,1,0:T(2,128)(2,1)S(1)} %collective-permute-done.3, bf16[1,2,6,1,3072]{4,3,2,1,0:T(2,128)(2,1)S(1)} %collective-permute-done.2, ...), kind=kLoop, calls=%fused_computation.18 | loop fusion | flops 5111808 | bytes 1044480 | tf_op jit(solution)/shard_map/convert_element_type | solution.py:458
  24.6 0.1 reshape.120.tile_ref
  24.7 0.0 copy-done
  24.7 0.0 copy-start.1
  24.7 1.3 %copy-done.1 = bf16[1,226,3072]{2,1,0:T(8,128)(2,1)S(1)} copy-done((bf16[1,226,3072]{2,1,0:T(8,128)(2,1)S(1)}, bf16[1,226,3072]{2,1,0:T(8,128)(2,1)}, u32[]{:S(2)}) %copy-start.1) | copy-done | bytes 1388568
  26.0 41.3 %shard_map.73 = bf16[128,512]{1,0:T(8,128)(2,1)S(1)} custom-call(s32[1]{0:T(128)S(6)} %copy.16.len_ref, bf16[32,3072]{1,0:T(8,128)(2,1)S(1)} %reshape.120.tile_ref, bf16[226,3072]{1,0:T(8,128)(2,1)S(1)} %bitcast.16, bf16[16,512]{1,0:T(8,128)(2,1)S(1)} %broadcast_in_dim.2.act_ref, bf16[512,1536]{1,0:T(8,128)(2,1)S(1)} %copy-done, ...), custom_call_target="tpu_custom_call" | custom-call | tf_op jit(solution)/shard_map/pallas_call | solution.py:473
  67.3 0.7 copy.18
  (5 shorter events, 0.1 us)
Async XLA Ops:
  0.9 11.2 %collective-permute-start = (bf16[1,2,1,4,3072]{4,3,2,1,0:T(4,128)(2,1)S(1)}, bf16[1,2,1,4,3072]{4,3,2,1,0:T(4,128)(2,1)S(1)}, u32[]{:S(2)}, u32[]{:S(2)}) collective-permute-start(bf16[1,2,1,4,3072]{4,3,2,1,0:T(4,128)(2,1)S(1)} %get-tuple-element.8), channel_id=1, source_target_pairs={{0,4},{4,8},{8,12},{1,5},{5,9},{9,13},{2,6},{6,10},{10,14},{3,7},{... | collective-permute-start | bytes 147464 | tf_op jit(solution)/shard_map/ppermute | solution.py:21
  5.7 6.5 %collective-permute-start.1 = (bf16[1,2,1,4,3072]{4,3,2,1,0:T(4,128)(2,1)S(1)}, bf16[1,2,1,4,3072]{4,3,2,1,0:T(4,128)(2,1)S(1)}, u32[]{:S(2)}, u32[]{:S(2)}) collective-permute-start(bf16[1,2,1,4,3072]{4,3,2,1,0:T(4,128)(2,1)S(1)} %get-tuple-element.7), channel_id=1, source_target_pairs={{4,0},{8,4},{12,8},{5,1},{9,5},{13,9},{6,2},{10,6},{14,10},{7,3},{... | collective-permute-start | bytes 147464 | tf_op jit(solution)/shard_map/ppermute | solution.py:24
  10.6 1.5 %copy-start.2 = (bf16[1,2,4,4,3072]{4,3,2,1,0:T(4,128)(2,1)S(1)}, bf16[1,2,4,4,3072]{4,3,2,1,0:T(4,128)(2,1)}, u32[]{:S(2)}) copy-start(bf16[1,2,4,4,3072]{4,3,2,1,0:T(4,128)(2,1)} %param.7) | copy-start | bytes 589828
  12.2 12.4 %copy-start = (bf16[512,1536]{1,0:T(8,128)(2,1)S(1)}, bf16[512,1536]{1,0:T(8,128)(2,1)}, u32[]{:S(2)}) copy-start(bf16[512,1536]{1,0:T(8,128)(2,1)} %mod_ref.1) | copy-start | bytes 4718596
  12.5 6.4 %collective-permute-start.2 = (bf16[1,2,6,1,3072]{4,3,2,1,0:T(2,128)(2,1)S(1)}, bf16[1,2,6,1,3072]{4,3,2,1,0:T(2,128)(2,1)S(1)}, u32[]{:S(2)}, u32[]{:S(2)}) collective-permute-start(bf16[1,2,6,1,3072]{4,3,2,1,0:T(2,128)(2,1)S(1)} %get-tuple-element.5), channel_id=1, source_target_pairs={{0,1},{1,2},{2,3},{4,5},{5,6},{6,7},{8,9},{9,10},{10,11},{12,13},{... | collective-permute-start | bytes 221192 | tf_op jit(solution)/shard_map/ppermute | solution.py:21
  16.1 7.0 %collective-permute-start.3 = (bf16[1,2,6,1,3072]{4,3,2,1,0:T(2,128)(2,1)S(1)}, bf16[1,2,6,1,3072]{4,3,2,1,0:T(2,128)(2,1)S(1)}, u32[]{:S(2)}, u32[]{:S(2)}) collective-permute-start(bf16[1,2,6,1,3072]{4,3,2,1,0:T(2,128)(2,1)S(1)} %get-tuple-element.6), channel_id=1, source_target_pairs={{1,0},{2,1},{3,2},{5,4},{6,5},{7,6},{9,8},{10,9},{11,10},{13,12},{... | collective-permute-start | bytes 221192 | tf_op jit(solution)/shard_map/ppermute | solution.py:24
  24.7 1.4 %copy-start.1 = (bf16[1,226,3072]{2,1,0:T(8,128)(2,1)S(1)}, bf16[1,226,3072]{2,1,0:T(8,128)(2,1)}, u32[]{:S(2)}) copy-start(bf16[1,226,3072]{2,1,0:T(8,128)(2,1)} %param.8) | copy-start | bytes 4165636

commit v2 on v1

--- a/solution.py
+++ b/solution.py
@@ -3,6 +3,7 @@
 
 import jax
 import jax.numpy as jnp
+import numpy as np
 from jax import lax
 from jax.experimental import pallas as pl
 from jax.experimental.pallas import tpu as pltpu
@@ -142,15 +143,73 @@
     return centered * lax.rsqrt(spread + 1e-06)
 
 
+SIDES = ((-1, 0), (1, 0), (0, -1), (0, 1), (-1, -1), (-1, 1), (1, -1), (1, 1))
+
+
+def halo_tables(frames, tile_h, tile_w, parts):
+    tokens = frames * tile_h * tile_w
+    edge = frames * tile_h
+
+    def token(f, h, w):
+        return (f * tile_h + h) * tile_w + w
+
+    pick = np.zeros((1 + parts, 64, tokens), np.float32)
+    shift = np.zeros((parts, 8 * tokens, tokens + 8 * edge + 64), np.float32)
+    last_h, last_w = tile_h - 1, tile_w - 1
+    for at, (down, right) in enumerate(SIDES):
+        h_from = last_h if down < 0 else 0
+        w_from = last_w if right < 0 else 0
+        for f in range(frames):
+            if at < 4:
+                for k in range(tile_h):
+                    source = token(f, h_from, k) if down else token(f, k, w_from)
+                    pick[0, at * edge + f * tile_h + k, source] = 1
+            else:
+                for part in range(parts):
+                    pick[1 + part, (at - 4) * 16 + part * frames + f, token(f, h_from, w_from)] = 1
+        for part in range(parts):
+            upper = part // (parts // 2)
+            for f in range(frames):
+                for h in range(tile_h):
+                    for w in range(tile_w):
+                        y, x = h + down, w + right
+                        out_y = -1 if y < 0 else (1 if y > last_h else 0)
+                        out_x = -1 if x < 0 else (1 if x > last_w else 0)
+                        if out_y == 0 and out_x == 0:
+                            source = token(f, y, x)
+                        else:
+                            slot = SIDES.index((out_y, out_x))
+                            if slot < 4:
+                                k = x if out_y else y
+                                source = tokens + slot * 2 * edge + upper * edge + f * tile_h + k
+                            else:
+                                source = tokens + 8 * edge + (slot - 4) * 16 + part * frames + f
+                        shift[part, at * tokens + token(f, h, w), source] = 1
+    return pick, shift
+
+
 def layer_kernel(
     sizes,
     len_ref,
     tile_ref,
-    prompt_ref,
+    pick_ref,
+    shift_ref,
+    peg_ref,
+    prompt_hbm,
     act_ref,
-    mod_ref,
+    mod_hbm,
     weight_ref,
     out_ref,
+    prompt_ref,
+    mod_ref,
+    side_send,
+    side_in,
+    corner_send,
+    corner_in,
+    conv,
+    local_sems,
+    halo_send,
+    halo_recv,
     mod_buf,
     affine,
     weights,
@@ -202,16 +261,71 @@
             src_ref=src, dst_ref=dst, send_sem=send, recv_sem=recv, device_id=where, device_id_type=MESH
         )
 
+    prompt_copy = pltpu.make_async_copy(prompt_hbm, prompt_ref, local_sems.at[0])
+    mod_copy = pltpu.make_async_copy(mod_hbm, mod_ref, local_sems.at[1])
+    mod_copy.start()
+    prompt_copy.start()
+    side_in[...] = jnp.zeros_like(side_in)
+    corner_in[...] = jnp.zeros_like(corner_in)
+
+    def within(down, right):
+        r, c = row + down, col + right
+        return (r >= 0) & (r < rows) & (c >= 0) & (c < cols)
+
     barrier = pltpu.get_barrier_semaphore()
+    for down, right in SIDES[4:]:
+
+        @pl.when(within(down, right))
+        def greet(down=down, right=right):
+            pl.semaphore_signal(
+                barrier, inc=1, device_id={"row": row + down, "col": col + right}, device_id_type=MESH
+            )
+
     pl.semaphore_signal(barrier, inc=1, device_id={"item": 1 - item}, device_id_type=MESH)
     for step in range(1, rows):
         pl.semaphore_signal(barrier, inc=1, device_id={"row": row_peer(step)}, device_id_type=MESH)
     for step in range(1, cols):
         pl.semaphore_signal(barrier, inc=1, device_id={"col": col_peer(step)}, device_id_type=MESH)
 
+    tile = tile_ref[...]
+    wide = side_in.shape[2]
+    narrow = corner_in.shape[1]
+    edge = side_in.shape[1] // 2
+    picked = jnp.dot(pick_ref[0, 0 : 4 * edge], tile, preferred_element_type=jnp.float32)
+    for side in range(4):
+        lines = picked[side * edge : (side + 1) * edge]
+        side_send[side] = jnp.concatenate([lines[:, :wide], lines[:, wide:]], axis=0).astype(jnp.bfloat16)
+    corners = jnp.zeros((corner_in.shape[0], narrow), jnp.float32)
+    for part in range(width // narrow):
+        corners = corners + jnp.dot(
+            pick_ref[1 + part],
+            tile[:, part * narrow : (part + 1) * narrow],
+            preferred_element_type=jnp.float32,
+        )
+    corner_send[...] = corners.astype(jnp.bfloat16)
+
+    def halo_copy(at, down, right):
+        if at < 4:
+            src, dst = side_send.at[at], side_in.at[at]
+        else:
+            lines = pl.ds((at - 4) * 16, 16)
+            src, dst = corner_send.at[lines, :], corner_in.at[lines, :]
+        return remote(
+            src, dst, halo_send.at[at], halo_recv.at[at], {"row": row - down, "col": col - right}
+        )
+
+    mod_copy.wait()
     own_columns = jnp.dot(act_ref[...], mod_ref[...], preferred_element_type=jnp.float32)
     mod_buf[col] = own_columns[0:1, :]
-    pl.semaphore_wait(barrier, rows + cols - 1)
+    beside_rows = (row + rows - 1) // rows + (2 * rows - 2 - row) // rows
+    beside_cols = (col + cols - 1) // cols + (2 * cols - 2 - col) // cols
+    pl.semaphore_wait(barrier, rows + cols - 1 + beside_rows * beside_cols)
+    for at, (down, right) in enumerate(SIDES):
+
+        @pl.when(within(-down, -right))
+        def send(at=at, down=down, right=right):
+            halo_copy(at, down, right).start()
+
     mod_copies = []
     for step in range(1, cols):
         copy = remote(
@@ -233,7 +347,29 @@
     weight_copy.start()
     for dest in range(rows):
         weights[dest, 0:depth, :] = weight_ref[dest]
-    tile_normal = centered_rows(tile_ref[...].astype(jnp.float32))
+    for at, (down, right) in enumerate(SIDES):
+
+        @pl.when(within(down, right))
+        def receive(at=at, down=down, right=right):
+            halo_copy(at, down, right).wait_recv()
+
+    for part in range(width // narrow):
+        lanes = slice(part * narrow, (part + 1) * narrow)
+        upper, start = divmod(part * narrow, wide)
+        pieces = [tile[:, lanes]]
+        for side in range(4):
+            pieces.append(side_in[side, :, start : start + narrow])
+        pieces.append(corner_in[...])
+        moved = jnp.dot(
+            shift_ref[part], jnp.concatenate(pieces, axis=0), preferred_element_type=jnp.float32
+        )
+        own = tile[:, lanes].astype(jnp.float32)
+        taps = [peg_ref[a, :, lanes].astype(jnp.float32) for a in range(3)]
+        summed = own + own * taps[1][1:2]
+        for at, (down, right) in enumerate(SIDES):
+            summed = summed + moved[at * tokens : (at + 1) * tokens] * taps[down + 1][right + 1 : right + 2]
+        conv[:, lanes] = summed.astype(jnp.bfloat16)
+    tile_normal = centered_rows(conv[...].astype(jnp.float32))
     for step in range(1, cols):
         remote(
             mod_buf.at[col],
@@ -316,6 +452,7 @@
 
     latent_part(0)
 
+    prompt_copy.wait()
     scale_pieces = [affine[1, :, pl.ds(start, depth)] for start in own_slices]
     shift_pieces = [affine[0, :, pl.ds(start, depth)] for start in own_slices]
     for start_row in range(0, padded_text, 16):
@@ -439,6 +576,12 @@
         ).wait_recv()
     for source in range(rows):
         out_ref[:, source * out_w : (source + 1) * out_w] = recv_out[source]
+    for at, (down, right) in enumerate(SIDES):
+
+        @pl.when(within(-down, -right))
+        def sent(at=at, down=down, right=right):
+            halo_copy(at, down, right).wait_send()
+
     for copy in mod_copies + [weight_copy] + x_copies + z_copies + p_copies + t_copies + o_copies:
         copy.wait_send()
 
@@ -447,22 +590,18 @@
     rows, cols, latents, prompt_rows, peg_weight, modulation_weight, qkv_weight, text_len, timestep
 ):
     frames, tile_h, tile_w, width = latents.shape[1:]
-    padded = with_halo(latents, (("row", 2), ("col", 3)), 1)
-    summed = latents.astype(jnp.float32)
-    for row_tap in range(3):
-        for col_tap in range(3):
-            summed = summed + padded[
-                :, :, row_tap : row_tap + tile_h, col_tap : col_tap + tile_w, :
-            ].astype(jnp.float32) * peg_weight[row_tap, col_tap].astype(jnp.float32)
     tokens = frames * tile_h * tile_w
-    tile = summed.astype(jnp.bfloat16).reshape(tokens, width)
+    tile = latents.reshape(tokens, width)
+    parts = 8
+    narrow = width // parts
+    pick, shift = (jnp.asarray(table, jnp.bfloat16) for table in halo_tables(frames, tile_h, tile_w, parts))
     temb = modulation_weight.shape[0]
     activation = jax.nn.silu(time_angles(timestep[0], temb)).astype(jnp.bfloat16)
     activation = jnp.broadcast_to(activation[None, :], (16, temb))
-    depth, parts, head_width = qkv_weight.shape
+    depth, kinds, head_width = qkv_weight.shape
     out_w = head_width // rows
-    by_dest = qkv_weight.reshape(depth, parts, rows, out_w).transpose(2, 0, 1, 3)
-    by_dest = by_dest.reshape(rows, depth, parts * out_w)
+    by_dest = qkv_weight.reshape(depth, kinds, rows, out_w).transpose(2, 0, 1, 3)
+    by_dest = by_dest.reshape(rows, depth, kinds * out_w)
     text = prompt_rows.shape[1]
     padded_text = -(-text // 16) * 16
     block = tokens * cols
@@ -473,21 +612,31 @@
     attended = pl.pallas_call(
         functools.partial(layer_kernel, (rows, cols, text, padded_text, tile_w)),
         out_shape=jax.ShapeDtypeStruct((block, head_width), bf16),
-        in_specs=[pl.BlockSpec(memory_space=pltpu.SMEM)] + [pl.BlockSpec(memory_space=VMEM)] * 5,
+        in_specs=[pl.BlockSpec(memory_space=pltpu.SMEM)] + [pl.BlockSpec(memory_space=space) for space in (VMEM,) * 4 + (pltpu.HBM, VMEM, pltpu.HBM, VMEM)],
         out_specs=pl.BlockSpec(memory_space=VMEM),
         scratch_shapes=[
+            VMEM((text, width), bf16),
+            VMEM(modulation_weight.shape, bf16),
+            VMEM((4, 16, width // 2), bf16),
+            VMEM((4, 16, width // 2), bf16),
+            VMEM((64, narrow), bf16),
+            VMEM((64, narrow), bf16),
+            VMEM((tokens, width), bf16),
+            dma((2,)),
+            dma((8,)),
+            dma((8,)),
             VMEM((cols, 1, modulation_weight.shape[1]), f32),
             VMEM((2, 1, width), f32),
-            VMEM((rows, 2 * depth, parts * out_w), bf16),
+            VMEM((rows, 2 * depth, kinds * out_w), bf16),
             VMEM((max(padded_text, tokens), width), bf16),
             VMEM((rows - 1, tokens, 2 * depth), bf16),
             VMEM((cols, group_rows, 2 * depth), bf16),
             VMEM((rows - 1, padded_text, 2 * out_w), bf16),
             VMEM((rows - 1, padded_text, 2 * out_w), bf16),
             VMEM((padded_text, 2 * out_w), f32),
-            VMEM((cols, rows - 1, group_rows, parts * out_w), bf16),
-            VMEM((cols, rows - 1, group_rows, parts * out_w), bf16),
-            VMEM((cols, group_rows, parts * out_w), f32),
+            VMEM((cols, rows - 1, group_rows, kinds * out_w), bf16),
+            VMEM((cols, rows - 1, group_rows, kinds * out_w), bf16),
+            VMEM((cols, group_rows, kinds * out_w), f32),
             VMEM((rows, block, out_w), bf16),
             VMEM((all_rows, out_w), bf16),
             VMEM((all_rows, out_w), bf16),
@@ -510,7 +659,7 @@
         compiler_params=pltpu.CompilerParams(
             collective_id=0, has_side_effects=True, vmem_limit_bytes=48 * 1024 * 1024
         ),
-    )(text_len, tile, prompt_rows[0], activation, modulation_weight, by_dest)
+    )(text_len, tile, pick, shift, peg_weight, prompt_rows[0], activation, modulation_weight, by_dest)
     return attended.reshape(1, frames, tile_h, tile_w * cols, head_width)
 
 
@@ -529,7 +678,7 @@
 
     def on_device(*blocks):
         group = blocks[4].shape[2] // rows
-        if items == 2 and cols % 2 == 0 and group >= 128 and group % 128 == 0:
+        if items == 2 and cols % 2 == 0 and group >= 128 and group % 128 == 0 and blocks[0].shape[1:4] == (2, 4, 4):
             return on_device_fast(rows, cols, *blocks)
         return on_device_general(*blocks)
 

time: 68.4 us -> 55.8 us (0.82)
  starting transfers between devices: 11 us -> 0 us
  waiting for transfers between devices: 5.72 us -> 0 us
  Pallas kernels: 41.3 us -> 46.1 us
  other arithmetic: 2.56 us -> 0.06 us
  local copies, waits for them, and re-layouts: 5.89 us -> 8.03 us
    ppermute x4 -> x0, starting transfers between devices: 11 us -> none  [the longest x2 8.47 us: with_halo(): lax.ppermute(lax.slice_in_dim(block, block.shape[dim] - width, None, axis...]
    ppermute x4 -> x0, waiting for transfers between devices: 5.72 us -> none  [the longest x2 4.24 us: with_halo(): lax.ppermute(lax.slice_in_dim(block, 0, width, axis=dim), axis, backward)]
    pallas_call x1, Pallas kernels: 41.3 us -> 46.1 us  [on_device_fast(): pl.pallas_call(functools.partial(layer_kernel, (rows, cols, text, padded_...]
    convert_element_type x2 -> x0, other arithmetic: 2.5 us -> none  [the longest x1 1.44 us: on_device_fast(): tile = summed.astype(jnp.bfloat16).reshape(tokens, width)]
    unnamed x10 -> x14, local copies, waits for them, and re-layouts: 3.83 us -> 4.95 us
    slice x2 -> x0, local copies, waits for them, and re-layouts: 1.07 us -> none  [the longest x1 0.86 us: with_halo(): lax.slice_in_dim(block, 0, width, axis=dim)]
    reshape x2, local copies, waits for them, and re-layouts: 0.84 us -> 1.9 us  [the longest x1 1.85 us: on_device_fast(): by_dest = by_dest.reshape(rows, depth, kinds * out_w)]
    transpose x1, local copies, waits for them, and re-layouts: 0.12 us -> 1.17 us  [on_device_fast(): qkv_weight.reshape(depth, kinds, rows, out_w).transpose(2, 0, 1, 3)]
  transfers between devices with their start and end apart: 4 -> 0, of which waited for: 2 -> 0; matrix products, arithmetic and copies ran while one was open for 6% -> 0% of each run, Pallas kernels for 0% -> 0%
where the time goes in v2:
time: 55.8 us; the launch traced here: 55.5 us
  Pallas kernels  46.1 us (83%)
  local copies, waits for them, and re-layouts  8.03 us (14%)
  between operations  1.39 us (2%)
    pallas_call x1, Pallas kernels, on_device_fast(): pl.pallas_call(functools.partial(layer_kernel, (rows, cols, text, padded_...  46.1 us
    unnamed x14, local copies, waits for them, and re-layouts  4.95 us
    reshape x1, local copies, waits for them, and re-layouts, on_device_fast(): by_dest = by_dest.reshape(rows, depth, kinds * out_w)  1.85 us
    transpose x1, local copies, waits for them, and re-layouts, on_device_fast(): qkv_weight.reshape(depth, kinds, rows, out_w).transpose(2, 0, 1, 3)  1.17 us

profile of v2, /device:TPU:0, one launch (start us, length us, event | category | flops | bytes accessed | tf_op | source)
XLA Modules:
  0.0 55.5 jit_solution(6529749132916001665)
XLA Ops:
  0.7 1.7 %copy.12 = bf16[384,3,512]{0,2,1:T(8,128)(2,1)S(1)} copy(bf16[384,3,512]{2,0,1:T(8,128)(2,1)} %param.13) | data formatting | bytes 2359296 | tf_op args[4]
  2.4 1.2 %copy.13 = bf16[4,384,3,128]{1,3,2,0:T(8,128)(2,1)} copy(bf16[4,384,3,128]{1,3,0,2:T(8,128)(2,1)S(1)} %bitcast.10) | data formatting | bytes 2359296 | tf_op jit(solution)/shard_map/transpose | solution.py:603
  3.6 0.0 copy-start.5
  3.6 0.0 copy-start
  3.6 0.0 copy-start.3
  3.6 0.0 copy-start.4
  3.6 1.9 %copy.14.weight_ref = bf16[4,384,384]{2,1,0:T(8,128)(2,1)S(1)} copy(bf16[4,384,384]{1,2,0:T(8,128)(2,1)} %bitcast.9) | data formatting | bytes 2359296 | tf_op jit(solution)/shard_map/reshape | solution.py:604
  5.5 0.0 copy-done.5
  6.2 0.0 copy-done
  6.2 0.0 copy-done.3
  6.2 0.0 copy-done.4
  6.2 0.0 copy-start.1
  6.2 1.3 %copy-done.1 = bf16[1,226,3072]{2,1,0:T(8,128)(2,1)S(1)} copy-done((bf16[1,226,3072]{2,1,0:T(8,128)(2,1)S(1)}, bf16[1,226,3072]{2,1,0:T(8,128)(2,1)}, u32[]{:S(2)}) %copy-start.1) | copy-done | bytes 1388568
  7.6 0.0 copy-start.2
  7.6 1.2 %copy-done.2 = bf16[8,256,160]{2,1,0:T(8,128)(2,1)S(1)} copy-done((bf16[8,256,160]{2,1,0:T(8,128)(2,1)S(1)}, bf16[8,256,160]{2,1,0:T(8,128)(2,1)}, u32[]{:S(2)}) %copy-start.2) | copy-done | bytes 655384
  8.8 46.1 %shard_map.91 = bf16[128,512]{1,0:T(8,128)(2,1)S(1)} custom-call(s32[1]{0:T(128)S(6)} %copy.16.len_ref, bf16[32,3072]{1,0:T(8,128)(2,1)S(1)} %reshape.39.tile_ref, bf16[9,64,32]{2,1,0:T(8,128)(2,1)S(1)} %copy-done.3, bf16[8,256,160]{2,1,0:T(8,128)(2,1)S(1)} %copy-done.2, bf16[3,3,3072]{2,1,0:T(4,128)(2,1)S(1)} %copy-done.4, bf16[226,3072]{1,0:T(8,128)(2,1)S(1)} %bitcast.7, ...), custom_call_target="tpu_custom_call" | custom-call | tf_op jit(solution)/shard_map/pallas_call | solution.py:612
  54.9 0.7 %copy.18 = bf16[1,2,4,16,512]{4,3,2,1,0:T(8,128)(2,1)} copy(bf16[1,2,4,16,512]{4,3,2,1,0:T(8,128)(2,1)S(1)} %bitcast.8) | data formatting | bytes 262144
  (4 shorter events, 0.1 us)
Async XLA Ops:
  3.6 1.9 %copy-start.5 = (bf16[1,2,4,4,3072]{4,3,2,1,0:T(4,128)(2,1)S(1)}, bf16[1,2,4,4,3072]{4,3,2,1,0:T(4,128)(2,1)}, u32[]{:S(2)}) copy-start(bf16[1,2,4,4,3072]{4,3,2,1,0:T(4,128)(2,1)} %param.9) | copy-start | bytes 589828
  3.6 2.6 %copy-start = (bf16[512,1536]{1,0:T(8,128)(2,1)S(1)}, bf16[512,1536]{1,0:T(8,128)(2,1)}, u32[]{:S(2)}) copy-start(bf16[512,1536]{1,0:T(8,128)(2,1)} %mod_hbm.1) | copy-start | bytes 4718596
  3.6 2.6 %copy-start.3 = (bf16[9,64,32]{2,1,0:T(8,128)(2,1)S(1)}, bf16[9,64,32]{2,1,0:T(8,128)(2,1)}, u32[]{:S(2)}) copy-start(bf16[9,64,32]{2,1,0:T(8,128)(2,1)} %constant.12.clone.pick_ref) | copy-start | bytes 110596
  3.6 2.6 %copy-start.4 = (bf16[3,3,3072]{2,1,0:T(4,128)(2,1)S(1)}, bf16[3,3,3072]{2,1,0:T(4,128)(2,1)}, u32[]{:S(2)}) copy-start(bf16[3,3,3072]{2,1,0:T(4,128)(2,1)} %peg_ref.1) | copy-start | bytes 165892
  6.2 1.4 %copy-start.1 = (bf16[1,226,3072]{2,1,0:T(8,128)(2,1)S(1)}, bf16[1,226,3072]{2,1,0:T(8,128)(2,1)}, u32[]{:S(2)}) copy-start(bf16[1,226,3072]{2,1,0:T(8,128)(2,1)} %param.10) | copy-start | bytes 4165636
  7.6 1.2 %copy-start.2 = (bf16[8,256,160]{2,1,0:T(8,128)(2,1)S(1)}, bf16[8,256,160]{2,1,0:T(8,128)(2,1)}, u32[]{:S(2)}) copy-start(bf16[8,256,160]{2,1,0:T(8,128)(2,1)} %constant.13.clone.shift_ref) | copy-start | bytes 1966084

commit v3 on v2

--- a/solution.py
+++ b/solution.py
@@ -347,6 +347,16 @@
     weight_copy.start()
     for dest in range(rows):
         weights[dest, 0:depth, :] = weight_ref[dest]
+    prompt_copy.wait()
+    text_stats = []
+    for start_row in range(0, padded_text, 16):
+        count = min(16, text - start_row)
+        values = prompt_ref[start_row : start_row + count, :].astype(jnp.float32)
+        center = jnp.mean(values, axis=-1, keepdims=True)
+        centered = values - center
+        spread = lax.rsqrt(jnp.mean(centered * centered, axis=-1, keepdims=True) + 1e-06)
+        text_stats.append((center, spread))
+
     for at, (down, right) in enumerate(SIDES):
 
         @pl.when(within(down, right))
@@ -399,7 +409,7 @@
             ]
         copy = remote(
             send_x.at[step - 1],
-            grid_x.at[0, pl.ds(pl.multiple_of(row * tokens, tokens), tokens), :],
+            grid_x.at[col, pl.ds(pl.multiple_of(row * tokens, tokens), tokens), :],
             x_send.at[step - 1],
             x_recv.at[step - 1],
             {"row": peer},
@@ -409,58 +419,16 @@
     own_slices = depth_slices(row)
     for order, start in enumerate(own_slices):
         grid_x[
-            0, pl.ds(pl.multiple_of(row * tokens, tokens), tokens), order * depth : (order + 1) * depth
+            col, pl.ds(pl.multiple_of(row * tokens, tokens), tokens), order * depth : (order + 1) * depth
         ] = text_in[0:tokens, pl.ds(start, depth)]
 
-    for step in range(1, rows):
-        source = lax.rem(row - step + rows, rows)
-        remote(
-            send_x.at[step - 1],
-            grid_x.at[0, pl.ds(pl.multiple_of(source * tokens, tokens), tokens), :],
-            x_send.at[step - 1],
-            x_recv.at[step - 1],
-            {"row": row_peer(step)},
-        ).wait_recv()
-    z_copies = []
-    for step in range(1, cols):
-        copy = remote(
-            grid_x.at[0], grid_x.at[step], z_send.at[step - 1], z_recv.at[step - 1], {"col": col_peer(step)}
-        )
-        copy.start()
-        z_copies.append(copy)
     weight_copy.wait_recv()
 
-    p_copies = []
-
-    def latent_part(group):
-        values = grid_x[group]
-        for step in range(1, rows):
-            peer = row_peer(step)
-            send_part[group, step - 1] = jnp.dot(
-                values, weights[peer], preferred_element_type=jnp.float32
-            ).astype(jnp.bfloat16)
-            copy = remote(
-                send_part.at[group, step - 1],
-                recv_part.at[group, step - 1],
-                p_send.at[group, step - 1],
-                p_recv.at[group, step - 1],
-                {"row": peer},
-            )
-            copy.start()
-            p_copies.append(copy)
-        own_part[group] = jnp.dot(values, weights[row], preferred_element_type=jnp.float32)
-
-    latent_part(0)
-
-    prompt_copy.wait()
     scale_pieces = [affine[1, :, pl.ds(start, depth)] for start in own_slices]
     shift_pieces = [affine[0, :, pl.ds(start, depth)] for start in own_slices]
     for start_row in range(0, padded_text, 16):
         count = min(16, text - start_row)
-        values = prompt_ref[start_row : start_row + count, :].astype(jnp.float32)
-        center = jnp.mean(values, axis=-1, keepdims=True)
-        centered = values - center
-        spread = lax.rsqrt(jnp.mean(centered * centered, axis=-1, keepdims=True) + 1e-06)
+        center, spread = text_stats[start_row // 16]
         for order, start in enumerate(own_slices):
             part = prompt_ref[start_row : start_row + count, pl.ds(start, depth)].astype(jnp.float32)
             normed = (part - center) * spread * scale_pieces[order] + shift_pieces[order]
@@ -487,9 +455,75 @@
         t_copies.append(copy)
     own_text[...] = jnp.dot(text_values, weights[row, :, out_w:], preferred_element_type=jnp.float32)
 
-    for group in range(1, cols):
-        z_copies[group - 1].wait_recv()
-        latent_part(group)
+    for step in range(1, rows):
+        source = lax.rem(row - step + rows, rows)
+        remote(
+            send_x.at[step - 1],
+            grid_x.at[col, pl.ds(pl.multiple_of(source * tokens, tokens), tokens), :],
+            x_send.at[step - 1],
+            x_recv.at[step - 1],
+            {"row": row_peer(step)},
+        ).wait_recv()
+    def z_copy(direction, distance, source):
+        sign = 1 - 2 * direction
+        return remote(
+            grid_x.at[source],
+            grid_x.at[source],
+            z_send.at[direction, distance - 1],
+            z_recv.at[direction, distance - 1],
+            {"col": col + sign},
+        )
+
+    def passes(direction, distance):
+        home = col - (distance - 1) * (1 - 2 * direction)
+        return (home >= 0) & (home < cols) & (col < cols - 1 if direction == 0 else col > 0)
+
+    def arrives(direction, distance):
+        home = col - distance * (1 - 2 * direction)
+        return (home >= 0) & (home < cols)
+
+    def pass_on(distance):
+        for direction in range(2):
+
+            @pl.when(passes(direction, distance))
+            def start(direction=direction):
+                z_copy(direction, distance, col - (distance - 1) * (1 - 2 * direction)).start()
+
+    pass_on(1)
+
+    def part_copy(group, step):
+        return remote(
+            send_part.at[group, step - 1],
+            recv_part.at[group, step - 1],
+            p_send.at[group, step - 1],
+            p_recv.at[group, step - 1],
+            {"row": row_peer(step)},
+        )
+
+    def latent_part(group):
+        values = grid_x[group]
+        for step in range(1, rows):
+            send_part[group, step - 1] = jnp.dot(
+                values, weights[row_peer(step)], preferred_element_type=jnp.float32
+            ).astype(jnp.bfloat16)
+            part_copy(group, step).start()
+        own_part[group] = jnp.dot(values, weights[row], preferred_element_type=jnp.float32)
+
+    latent_part(col)
+    for distance in range(1, cols):
+        for direction in range(2):
+
+            @pl.when(arrives(direction, distance))
+            def landed(direction=direction, distance=distance):
+                z_copy(direction, distance, col - distance * (1 - 2 * direction)).wait_recv()
+
+        if distance < cols - 1:
+            pass_on(distance + 1)
+        for direction in range(2):
+
+            @pl.when(arrives(direction, distance))
+            def multiply(direction=direction, distance=distance):
+                latent_part(col - distance * (1 - 2 * direction))
 
     for copy in t_copies:
         copy.wait_recv()
@@ -500,7 +534,7 @@
     v_buf[0:padded_text, :] = total[:, out_w:].astype(jnp.bfloat16)
     for group in range(cols):
         for step in range(1, rows):
-            p_copies[group * (rows - 1) + step - 1].wait_recv()
+            part_copy(group, step).wait_recv()
         total = own_part[group]
         for step in range(1, rows):
             total = total + recv_part[group, step - 1].astype(jnp.float32)
@@ -520,9 +554,7 @@
     token = source - group * tokens
     line = token // tile_w
     place = token - line * tile_w
-    owner = col - group
-    owner = jnp.where(owner < 0, owner + cols, owner)
-    target = (line * cols + owner) * tile_w + place
+    target = (line * cols + group) * tile_w + place
     permute = jnp.where(at == target, 1.0, 0.0).astype(jnp.bfloat16)
     keys = k_buf[...]
     vals = v_buf[...]
@@ -582,7 +614,17 @@
         def sent(at=at, down=down, right=right):
             halo_copy(at, down, right).wait_send()
 
-    for copy in mod_copies + [weight_copy] + x_copies + z_copies + p_copies + t_copies + o_copies:
+    for direction in range(2):
+        for distance in range(1, cols):
+
+            @pl.when(passes(direction, distance))
+            def passed(direction=direction, distance=distance):
+                z_copy(direction, distance, col - (distance - 1) * (1 - 2 * direction)).wait_send()
+
+    for group in range(cols):
+        for step in range(1, rows):
+            part_copy(group, step).wait_send()
+    for copy in mod_copies + [weight_copy] + x_copies + t_copies + o_copies:
         copy.wait_send()
 
 
@@ -647,8 +689,8 @@
             dma((cols - 1,)),
             dma((rows - 1,)),
             dma((rows - 1,)),
-            dma((cols - 1,)),
-            dma((cols - 1,)),
+            dma((2, cols - 1)),
+            dma((2, cols - 1)),
             dma((rows - 1,)),
             dma((rows - 1,)),
             dma((cols, rows - 1)),

time: 55.8 us -> 54.4 us (0.975)
  Pallas kernels: 46.1 us -> 44.7 us
    pallas_call x1, Pallas kernels: 46.1 us -> 44.7 us  [on_device_fast(): pl.pallas_call(functools.partial(layer_kernel, (rows, cols, text, padded_...]
where the time goes in v3:
time: 54.4 us; the launch traced here: 54.2 us
  Pallas kernels  44.7 us (82%)
  local copies, waits for them, and re-layouts  8.03 us (15%)
  between operations  1.39 us (3%)
    pallas_call x1, Pallas kernels, on_device_fast(): pl.pallas_call(functools.partial(layer_kernel, (rows, cols, text, padded_...  44.7 us
    unnamed x14, local copies, waits for them, and re-layouts  4.95 us
    reshape x1, local copies, waits for them, and re-layouts, on_device_fast(): by_dest = by_dest.reshape(rows, depth, kinds * out_w)  1.85 us
    transpose x1, local copies, waits for them, and re-layouts, on_device_fast(): qkv_weight.reshape(depth, kinds, rows, out_w).transpose(2, 0, 1, 3)  1.17 us

profile of v3, /device:TPU:0, one launch (start us, length us, event | category | flops | bytes accessed | tf_op | source)
XLA Modules:
  0.0 54.2 jit_solution(587528274755764546)
XLA Ops:
  0.7 1.7 %copy.12 = bf16[384,3,512]{0,2,1:T(8,128)(2,1)S(1)} copy(bf16[384,3,512]{2,0,1:T(8,128)(2,1)} %param.13) | data formatting | bytes 2359296 | tf_op args[4]
  2.4 1.2 %copy.13 = bf16[4,384,3,128]{1,3,2,0:T(8,128)(2,1)} copy(bf16[4,384,3,128]{1,3,0,2:T(8,128)(2,1)S(1)} %bitcast.10) | data formatting | bytes 2359296 | tf_op jit(solution)/shard_map/transpose | solution.py:645
  3.6 0.0 copy-start.5
  3.6 0.0 copy-start
  3.6 0.0 copy-start.3
  3.6 0.0 copy-start.4
  3.6 1.9 %copy.14.weight_ref = bf16[4,384,384]{2,1,0:T(8,128)(2,1)S(1)} copy(bf16[4,384,384]{1,2,0:T(8,128)(2,1)} %bitcast.9) | data formatting | bytes 2359296 | tf_op jit(solution)/shard_map/reshape | solution.py:646
  5.5 0.0 copy-done.5
  6.2 0.0 copy-done
  6.2 0.0 copy-done.3
  6.2 0.0 copy-done.4
  6.2 0.0 copy-start.1
  6.2 1.3 %copy-done.1 = bf16[1,226,3072]{2,1,0:T(8,128)(2,1)S(1)} copy-done((bf16[1,226,3072]{2,1,0:T(8,128)(2,1)S(1)}, bf16[1,226,3072]{2,1,0:T(8,128)(2,1)}, u32[]{:S(2)}) %copy-start.1) | copy-done | bytes 1388568
  7.6 0.0 copy-start.2
  7.6 1.2 %copy-done.2 = bf16[8,256,160]{2,1,0:T(8,128)(2,1)S(1)} copy-done((bf16[8,256,160]{2,1,0:T(8,128)(2,1)S(1)}, bf16[8,256,160]{2,1,0:T(8,128)(2,1)}, u32[]{:S(2)}) %copy-start.2) | copy-done | bytes 655384
  8.8 44.7 %shard_map.91 = bf16[128,512]{1,0:T(8,128)(2,1)S(1)} custom-call(s32[1]{0:T(128)S(6)} %copy.16.len_ref, bf16[32,3072]{1,0:T(8,128)(2,1)S(1)} %reshape.39.tile_ref, bf16[9,64,32]{2,1,0:T(8,128)(2,1)S(1)} %copy-done.3, bf16[8,256,160]{2,1,0:T(8,128)(2,1)S(1)} %copy-done.2, bf16[3,3,3072]{2,1,0:T(4,128)(2,1)S(1)} %copy-done.4, bf16[226,3072]{1,0:T(8,128)(2,1)S(1)} %bitcast.7, ...), custom_call_target="tpu_custom_call" | custom-call | tf_op jit(solution)/shard_map/pallas_call | solution.py:654
  53.5 0.7 %copy.18 = bf16[1,2,4,16,512]{4,3,2,1,0:T(8,128)(2,1)} copy(bf16[1,2,4,16,512]{4,3,2,1,0:T(8,128)(2,1)S(1)} %bitcast.8) | data formatting | bytes 262144
  (4 shorter events, 0.1 us)
Async XLA Ops:
  3.6 1.9 %copy-start.5 = (bf16[1,2,4,4,3072]{4,3,2,1,0:T(4,128)(2,1)S(1)}, bf16[1,2,4,4,3072]{4,3,2,1,0:T(4,128)(2,1)}, u32[]{:S(2)}) copy-start(bf16[1,2,4,4,3072]{4,3,2,1,0:T(4,128)(2,1)} %param.9) | copy-start | bytes 589828
  3.6 2.6 %copy-start = (bf16[512,1536]{1,0:T(8,128)(2,1)S(1)}, bf16[512,1536]{1,0:T(8,128)(2,1)}, u32[]{:S(2)}) copy-start(bf16[512,1536]{1,0:T(8,128)(2,1)} %mod_hbm.1) | copy-start | bytes 4718596
  3.6 2.6 %copy-start.3 = (bf16[9,64,32]{2,1,0:T(8,128)(2,1)S(1)}, bf16[9,64,32]{2,1,0:T(8,128)(2,1)}, u32[]{:S(2)}) copy-start(bf16[9,64,32]{2,1,0:T(8,128)(2,1)} %constant.12.clone.pick_ref) | copy-start | bytes 110596
  3.6 2.6 %copy-start.4 = (bf16[3,3,3072]{2,1,0:T(4,128)(2,1)S(1)}, bf16[3,3,3072]{2,1,0:T(4,128)(2,1)}, u32[]{:S(2)}) copy-start(bf16[3,3,3072]{2,1,0:T(4,128)(2,1)} %peg_ref.1) | copy-start | bytes 165892
  6.2 1.4 %copy-start.1 = (bf16[1,226,3072]{2,1,0:T(8,128)(2,1)S(1)}, bf16[1,226,3072]{2,1,0:T(8,128)(2,1)}, u32[]{:S(2)}) copy-start(bf16[1,226,3072]{2,1,0:T(8,128)(2,1)} %param.10) | copy-start | bytes 4165636
  7.6 1.2 %copy-start.2 = (bf16[8,256,160]{2,1,0:T(8,128)(2,1)S(1)}, bf16[8,256,160]{2,1,0:T(8,128)(2,1)}, u32[]{:S(2)}) copy-start(bf16[8,256,160]{2,1,0:T(8,128)(2,1)} %constant.13.clone.shift_ref) | copy-start | bytes 1966084

commit v4 on v3

--- a/solution.py
+++ b/solution.py
@@ -193,13 +193,14 @@
     len_ref,
     tile_ref,
     pick_ref,
-    shift_ref,
+    shift_hbm,
     peg_ref,
     prompt_hbm,
     act_ref,
     mod_hbm,
-    weight_ref,
+    weight_hbm,
     out_ref,
+    shift_ref,
     prompt_ref,
     mod_ref,
     side_send,
@@ -243,8 +244,8 @@
 ):
     rows, cols, text, padded_text, tile_w = sizes
     tokens, width = tile_ref.shape
-    depth = weight_ref.shape[1]
-    out_w = weight_ref.shape[2] // 3
+    depth = weight_hbm.shape[1]
+    out_w = weight_hbm.shape[2] // rows
     block = tokens * cols
     item = lax.axis_index("item")
     row = lax.axis_index("row")
@@ -263,8 +264,22 @@
 
     prompt_copy = pltpu.make_async_copy(prompt_hbm, prompt_ref, local_sems.at[0])
     mod_copy = pltpu.make_async_copy(mod_hbm, mod_ref, local_sems.at[1])
+    shift_copy = pltpu.make_async_copy(shift_hbm, shift_ref, local_sems.at[2])
+    stage_copies = []
+    for kind in range(3):
+        for dest in range(rows):
+            stage_copies.append(
+                pltpu.make_async_copy(
+                    weight_hbm.at[kind, :, dest * out_w : (dest + 1) * out_w],
+                    weights.at[dest, 0:depth, kind * out_w : (kind + 1) * out_w],
+                    local_sems.at[3 + kind * rows + dest],
+                )
+            )
     mod_copy.start()
+    for copy in stage_copies:
+        copy.start()
     prompt_copy.start()
+    shift_copy.start()
     side_in[...] = jnp.zeros_like(side_in)
     corner_in[...] = jnp.zeros_like(corner_in)
 
@@ -337,16 +352,16 @@
         )
         copy.start()
         mod_copies.append(copy)
+    for copy in stage_copies:
+        copy.wait()
     weight_copy = remote(
-        weight_ref,
+        weights.at[:, 0:depth, :],
         weights.at[:, pl.ds(depth, depth), :],
         w_sems.at[0],
         w_sems.at[1],
         {"item": 1 - item},
     )
     weight_copy.start()
-    for dest in range(rows):
-        weights[dest, 0:depth, :] = weight_ref[dest]
     prompt_copy.wait()
     text_stats = []
     for start_row in range(0, padded_text, 16):
@@ -363,6 +378,7 @@
         def receive(at=at, down=down, right=right):
             halo_copy(at, down, right).wait_recv()
 
+    shift_copy.wait()
     for part in range(width // narrow):
         lanes = slice(part * narrow, (part + 1) * narrow)
         upper, start = divmod(part * narrow, wide)
@@ -642,8 +658,7 @@
     activation = jnp.broadcast_to(activation[None, :], (16, temb))
     depth, kinds, head_width = qkv_weight.shape
     out_w = head_width // rows
-    by_dest = qkv_weight.reshape(depth, kinds, rows, out_w).transpose(2, 0, 1, 3)
-    by_dest = by_dest.reshape(rows, depth, kinds * out_w)
+    by_kind = qkv_weight.transpose(1, 0, 2)
     text = prompt_rows.shape[1]
     padded_text = -(-text // 16) * 16
     block = tokens * cols
@@ -654,9 +669,10 @@
     attended = pl.pallas_call(
         functools.partial(layer_kernel, (rows, cols, text, padded_text, tile_w)),
         out_shape=jax.ShapeDtypeStruct((block, head_width), bf16),
-        in_specs=[pl.BlockSpec(memory_space=pltpu.SMEM)] + [pl.BlockSpec(memory_space=space) for space in (VMEM,) * 4 + (pltpu.HBM, VMEM, pltpu.HBM, VMEM)],
+        in_specs=[pl.BlockSpec(memory_space=pltpu.SMEM)] + [pl.BlockSpec(memory_space=space) for space in (VMEM, VMEM, pltpu.HBM, VMEM, pltpu.HBM, VMEM, pltpu.HBM, pltpu.HBM)],
         out_specs=pl.BlockSpec(memory_space=VMEM),
         scratch_shapes=[
+            VMEM(shift.shape, bf16),
             VMEM((text, width), bf16),
             VMEM(modulation_weight.shape, bf16),
             VMEM((4, 16, width // 2), bf16),
@@ -664,7 +680,7 @@
             VMEM((64, narrow), bf16),
             VMEM((64, narrow), bf16),
             VMEM((tokens, width), bf16),
-            dma((2,)),
+            dma((3 + 3 * rows,)),
             dma((8,)),
             dma((8,)),
             VMEM((cols, 1, modulation_weight.shape[1]), f32),
@@ -699,9 +715,9 @@
             dma((rows - 1,)),
         ],
         compiler_params=pltpu.CompilerParams(
-            collective_id=0, has_side_effects=True, vmem_limit_bytes=48 * 1024 * 1024
+            collective_id=0, has_side_effects=True, vmem_limit_bytes=58 * 1024 * 1024
         ),
-    )(text_len, tile, pick, shift, peg_weight, prompt_rows[0], activation, modulation_weight, by_dest)
+    )(text_len, tile, pick, shift, peg_weight, prompt_rows[0], activation, modulation_weight, by_kind)
     return attended.reshape(1, frames, tile_h, tile_w * cols, head_width)
 
 

time: 54.4 us -> 51.6 us (0.949)
  local copies, waits for them, and re-layouts: 8.03 us -> 3.84 us
  Pallas kernels: 44.7 us -> 46.2 us
    unnamed x14 -> x1, local copies, waits for them, and re-layouts: 4.95 us -> 1.57 us
    reshape x1 -> x0, local copies, waits for them, and re-layouts: 1.85 us -> none  [on_device_fast(): by_dest = by_dest.reshape(rows, depth, kinds * out_w)]
    reshape x1, local copies, waits for them, and re-layouts: 0.05 us -> 1.65 us  [on_device_fast(): tile = latents.reshape(tokens, width)]
    pallas_call x1, Pallas kernels: 44.7 us -> 46.2 us  [on_device_fast(): pl.pallas_call(functools.partial(layer_kernel, (rows, cols, text, padded_...]
    transpose x1 -> x0, local copies, waits for them, and re-layouts: 1.17 us -> none  [on_device_fast(): qkv_weight.reshape(depth, kinds, rows, out_w).transpose(2, 0, 1, 3)]
    broadcast_in_dim x1, local copies, waits for them, and re-layouts: 0.01 us -> 0.62 us  [on_device_fast(): activation = jnp.broadcast_to(activation[None, :], (16, temb))]
where the time goes in v4:
time: 51.6 us; the launch traced here: 51.4 us
  Pallas kernels  46.2 us (90%)
  local copies, waits for them, and re-layouts  3.84 us (7%)
  between operations  1.32 us (3%)
    pallas_call x1, Pallas kernels, on_device_fast(): pl.pallas_call(functools.partial(layer_kernel, (rows, cols, text, padded_...  46.2 us
    reshape x1, local copies, waits for them, and re-layouts, on_device_fast(): tile = latents.reshape(tokens, width)  1.65 us
    unnamed x1, local copies, waits for them, and re-layouts  1.57 us

profile of v4, /device:TPU:0, one launch (start us, length us, event | category | flops | bytes accessed | tf_op | source)
XLA Modules:
  0.0 51.4 jit_solution(8082736744416330496)
XLA Ops:
  1.4 0.6 %broadcast_in_dim.2.act_ref = bf16[16,512]{1,0:T(8,128)(2,1)} broadcast(bf16[512]{0:T(512)(128)(2,1)S(1)} %fusion), dimensions={1} | broadcast | bytes 17408 | tf_op jit(solution)/shard_map/broadcast_in_dim | solution.py:658
  2.0 1.6 %reshape.33.tile_ref = bf16[32,3072]{1,0:T(8,128)(2,1)} reshape(bf16[1,2,4,4,3072]{4,3,2,1,0:T(4,128)(2,1)} %param.9) | data formatting | bytes 393216 | tf_op jit(solution)/shard_map/reshape | solution.py:652
  3.6 46.2 %shard_map.91 = bf16[128,512]{1,0:T(8,128)(2,1)} custom-call(s32[1]{0:T(128)S(6)} %copy.11.len_ref, bf16[32,3072]{1,0:T(8,128)(2,1)} %reshape.33.tile_ref, bf16[9,64,32]{2,1,0:T(8,128)(2,1)} %constant.12.clone.pick_ref, bf16[8,256,160]{2,1,0:T(8,128)(2,1)} %constant.13.clone.shift_hbm, bf16[3,3,3072]{2,1,0:T(4,128)(2,1)} %peg_ref.1, ...), custom_call_target="tpu_custom_call" | custom-call | tf_op jit(solution)/shard_map/pallas_call | solution.py:669
  49.8 1.6 %copy.13 = bf16[1,2,4,16,512]{4,3,2,1,0:T(8,128)(2,1)} copy(bf16[1,2,4,16,512]{4,3,2,1,0:T(8,128)(2,1)} %bitcast.6) | data formatting | bytes 262144
  (2 shorter events, 0.1 us)

commit v5 on v4

--- a/solution.py
+++ b/solution.py
@@ -217,12 +217,19 @@
     text_in,
     send_x,
     grid_x,
-    send_text,
-    recv_text,
+    tile_buf,
     own_text,
-    send_part,
-    recv_part,
+    text_first,
+    text_first_in,
+    text_hold,
+    text_second,
+    text_second_in,
     own_part,
+    part_first,
+    part_first_in,
+    part_hold,
+    part_second,
+    part_second_in,
     q_buf,
     k_buf,
     v_buf,
@@ -235,15 +242,13 @@
     x_recv,
     z_send,
     z_recv,
-    t_send,
-    t_recv,
-    p_send,
-    p_recv,
+    t_sems,
+    p_sems,
     o_send,
     o_recv,
 ):
     rows, cols, text, padded_text, tile_w = sizes
-    tokens, width = tile_ref.shape
+    tokens, width = tile_buf.shape
     depth = weight_hbm.shape[1]
     out_w = weight_hbm.shape[2] // rows
     block = tokens * cols
@@ -287,6 +292,66 @@
         r, c = row + down, col + right
         return (r >= 0) & (r < rows) & (c >= 0) & (c < cols)
 
+    near = (row + 1 - 2 * lax.rem(row, 2), row + 2 - 4 * lax.div(row, 2))
+    across = 3 - row
+
+    def first_copy(group, way, sems, first, first_in):
+        return remote(
+            first.at[group, way],
+            first_in.at[group, way],
+            sems.at[0, group, way],
+            sems.at[1, group, way],
+            {"row": near[way]},
+        )
+
+    def second_copy(group, way, sems, second, second_in):
+        return remote(
+            second.at[group, way],
+            second_in.at[group, way],
+            sems.at[2, group, way],
+            sems.at[3, group, way],
+            {"row": near[1 - way]},
+        )
+
+    def scatter_start(group, values, lane, own, first, first_in, hold, second, second_in, sems):
+        def product(dest):
+            return jnp.dot(values, weights[dest, :, lane:], preferred_element_type=jnp.float32)
+
+        half = values.shape[0] // 2
+        far = product(across)
+        for way in range(2):
+            first[group, way, 1] = far[way * half : (way + 1) * half].astype(jnp.bfloat16)
+        for way in range(2):
+            part = product(near[way])
+            first[group, way, 0] = part[way * half : (way + 1) * half].astype(jnp.bfloat16)
+            hold[group, 1 - way] = part[(1 - way) * half : (2 - way) * half]
+            first_copy(group, way, sems, first, first_in).start()
+        own[group] = product(row)
+
+    def scatter_pass(group, own, first, first_in, hold, second, second_in, sems):
+        half = hold.shape[2]
+        for way in range(2):
+            first_copy(group, way, sems, first, first_in).wait_recv()
+            second[group, way] = (
+                hold[group, way] + first_in[group, way, 1].astype(jnp.float32)
+            ).astype(jnp.bfloat16)
+            second_copy(group, way, sems, second, second_in).start()
+            lines = slice(way * half, (way + 1) * half)
+            own[group, lines] = own[group, lines] + first_in[group, way, 0].astype(jnp.float32)
+
+    def scatter_end(group, own, first, first_in, hold, second, second_in, sems):
+        sums = []
+        half = hold.shape[2]
+        for way in range(2):
+            second_copy(group, way, sems, second, second_in).wait_recv()
+            sums.append(
+                own[group, way * half : (way + 1) * half] + second_in[group, way].astype(jnp.float32)
+            )
+        return jnp.concatenate(sums, axis=0).astype(jnp.bfloat16)
+
+    text_state = (own_text, text_first, text_first_in, text_hold, text_second, text_second_in, t_sems)
+    part_state = (own_part, part_first, part_first_in, part_hold, part_second, part_second_in, p_sems)
+
     barrier = pltpu.get_barrier_semaphore()
     for down, right in SIDES[4:]:
 
@@ -302,7 +367,13 @@
     for step in range(1, cols):
         pl.semaphore_signal(barrier, inc=1, device_id={"col": col_peer(step)}, device_id_type=MESH)
 
-    tile = tile_ref[...]
+    pieces = [
+        tile_ref[0, f, h].astype(jnp.float32)
+        for f in range(tile_ref.shape[1])
+        for h in range(tile_ref.shape[2])
+    ]
+    tile_buf[...] = jnp.concatenate(pieces, axis=0).astype(jnp.bfloat16)
+    tile = tile_buf[...]
     wide = side_in.shape[2]
     narrow = corner_in.shape[1]
     edge = side_in.shape[1] // 2
@@ -366,6 +437,8 @@
     text_stats = []
     for start_row in range(0, padded_text, 16):
         count = min(16, text - start_row)
+        if count <= 0:
+            continue
         values = prompt_ref[start_row : start_row + count, :].astype(jnp.float32)
         center = jnp.mean(values, axis=-1, keepdims=True)
         centered = values - center
@@ -444,6 +517,9 @@
     shift_pieces = [affine[0, :, pl.ds(start, depth)] for start in own_slices]
     for start_row in range(0, padded_text, 16):
         count = min(16, text - start_row)
+        if count <= 0:
+            text_in[start_row : start_row + 16, 0 : 2 * depth] = jnp.zeros((16, 2 * depth), jnp.bfloat16)
+            continue
         center, spread = text_stats[start_row // 16]
         for order, start in enumerate(own_slices):
             part = prompt_ref[start_row : start_row + count, pl.ds(start, depth)].astype(jnp.float32)
@@ -454,22 +530,7 @@
                 jnp.bfloat16
             )
     text_values = text_in[:, 0 : 2 * depth]
-    t_copies = []
-    for step in range(1, rows):
-        peer = row_peer(step)
-        send_text[step - 1] = jnp.dot(
-            text_values, weights[peer, :, out_w:], preferred_element_type=jnp.float32
-        ).astype(jnp.bfloat16)
-        copy = remote(
-            send_text.at[step - 1],
-            recv_text.at[step - 1],
-            t_send.at[step - 1],
-            t_recv.at[step - 1],
-            {"row": peer},
-        )
-        copy.start()
-        t_copies.append(copy)
-    own_text[...] = jnp.dot(text_values, weights[row, :, out_w:], preferred_element_type=jnp.float32)
+    scatter_start(0, text_values, out_w, *text_state)
 
     for step in range(1, rows):
         source = lax.rem(row - step + rows, rows)
@@ -507,26 +568,20 @@
 
     pass_on(1)
 
-    def part_copy(group, step):
-        return remote(
-            send_part.at[group, step - 1],
-            recv_part.at[group, step - 1],
-            p_send.at[group, step - 1],
-            p_recv.at[group, step - 1],
-            {"row": row_peer(step)},
-        )
-
-    def latent_part(group):
-        values = grid_x[group]
-        for step in range(1, rows):
-            send_part[group, step - 1] = jnp.dot(
-                values, weights[row_peer(step)], preferred_element_type=jnp.float32
-            ).astype(jnp.bfloat16)
-            part_copy(group, step).start()
-        own_part[group] = jnp.dot(values, weights[row], preferred_element_type=jnp.float32)
-
-    latent_part(col)
+    def pass_sums(distance):
+        for direction in range(2):
+
+            @pl.when(arrives(direction, distance))
+            def forward(direction=direction):
+                scatter_pass(col - distance * (1 - 2 * direction), *part_state)
+
+    scatter_start(col, grid_x[col], 0, *part_state)
+    scatter_pass(0, *text_state)
     for distance in range(1, cols):
+        if distance == 1:
+            scatter_pass(col, *part_state)
+        else:
+            pass_sums(distance - 1)
         for direction in range(2):
 
             @pl.when(arrives(direction, distance))
@@ -539,22 +594,16 @@
 
             @pl.when(arrives(direction, distance))
             def multiply(direction=direction, distance=distance):
-                latent_part(col - distance * (1 - 2 * direction))
-
-    for copy in t_copies:
-        copy.wait_recv()
-    total = own_text[...]
-    for step in range(1, rows):
-        total = total + recv_text[step - 1].astype(jnp.float32)
-    k_buf[0:padded_text, :] = total[:, 0:out_w].astype(jnp.bfloat16)
-    v_buf[0:padded_text, :] = total[:, out_w:].astype(jnp.bfloat16)
+                group = col - distance * (1 - 2 * direction)
+                scatter_start(group, grid_x[group], 0, *part_state)
+
+    pass_sums(cols - 1)
+
+    rounded = scatter_end(0, *text_state)
+    k_buf[0:padded_text, :] = rounded[:, 0:out_w]
+    v_buf[0:padded_text, :] = rounded[:, out_w:]
     for group in range(cols):
-        for step in range(1, rows):
-            part_copy(group, step).wait_recv()
-        total = own_part[group]
-        for step in range(1, rows):
-            total = total + recv_part[group, step - 1].astype(jnp.float32)
-        rounded = total.astype(jnp.bfloat16)
+        rounded = scatter_end(group, *part_state)
         per_col = rows * tokens
         base = padded_text + group * per_col
         k_buf[base : base + per_col, :] = rounded[:, out_w : 2 * out_w]
@@ -637,10 +686,13 @@
             def passed(direction=direction, distance=distance):
                 z_copy(direction, distance, col - (distance - 1) * (1 - 2 * direction)).wait_send()
 
-    for group in range(cols):
-        for step in range(1, rows):
-            part_copy(group, step).wait_send()
-    for copy in mod_copies + [weight_copy] + x_copies + t_copies + o_copies:
+    for count, state in ((1, text_state), (cols, part_state)):
+        own, first, first_in, hold, second, second_in, sems = state
+        for group in range(count):
+            for way in range(2):
+                first_copy(group, way, sems, first, first_in).wait_send()
+                second_copy(group, way, sems, second, second_in).wait_send()
+    for copy in mod_copies + [weight_copy] + x_copies + o_copies:
         copy.wait_send()
 
 
@@ -649,7 +701,6 @@
 ):
     frames, tile_h, tile_w, width = latents.shape[1:]
     tokens = frames * tile_h * tile_w
-    tile = latents.reshape(tokens, width)
     parts = 8
     narrow = width // parts
     pick, shift = (jnp.asarray(table, jnp.bfloat16) for table in halo_tables(frames, tile_h, tile_w, parts))
@@ -660,7 +711,7 @@
     out_w = head_width // rows
     by_kind = qkv_weight.transpose(1, 0, 2)
     text = prompt_rows.shape[1]
-    padded_text = -(-text // 16) * 16
+    padded_text = -(-text // 32) * 32
     block = tokens * cols
     group_rows = tokens * rows
     bf16, f32 = jnp.bfloat16, jnp.float32
@@ -689,12 +740,19 @@
             VMEM((max(padded_text, tokens), width), bf16),
             VMEM((rows - 1, tokens, 2 * depth), bf16),
             VMEM((cols, group_rows, 2 * depth), bf16),
-            VMEM((rows - 1, padded_text, 2 * out_w), bf16),
-            VMEM((rows - 1, padded_text, 2 * out_w), bf16),
-            VMEM((padded_text, 2 * out_w), f32),
-            VMEM((cols, rows - 1, group_rows, kinds * out_w), bf16),
-            VMEM((cols, rows - 1, group_rows, kinds * out_w), bf16),
+            VMEM((tokens, width), bf16),
+            VMEM((1, padded_text, 2 * out_w), f32),
+            VMEM((1, 2, 2, padded_text // 2, 2 * out_w), bf16),
+            VMEM((1, 2, 2, padded_text // 2, 2 * out_w), bf16),
+            VMEM((1, 2, padded_text // 2, 2 * out_w), f32),
+            VMEM((1, 2, padded_text // 2, 2 * out_w), bf16),
+            VMEM((1, 2, padded_text // 2, 2 * out_w), bf16),
             VMEM((cols, group_rows, kinds * out_w), f32),
+            VMEM((cols, 2, 2, group_rows // 2, kinds * out_w), bf16),
+            VMEM((cols, 2, 2, group_rows // 2, kinds * out_w), bf16),
+            VMEM((cols, 2, group_rows // 2, kinds * out_w), f32),
+            VMEM((cols, 2, group_rows // 2, kinds * out_w), bf16),
+            VMEM((cols, 2, group_rows // 2, kinds * out_w), bf16),
             VMEM((rows, block, out_w), bf16),
             VMEM((all_rows, out_w), bf16),
             VMEM((all_rows, out_w), bf16),
@@ -707,17 +765,15 @@
             dma((rows - 1,)),
             dma((2, cols - 1)),
             dma((2, cols - 1)),
-            dma((rows - 1,)),
-            dma((rows - 1,)),
-            dma((cols, rows - 1)),
-            dma((cols, rows - 1)),
+            dma((4, 1, 2)),
+            dma((4, cols, 2)),
             dma((rows - 1,)),
             dma((rows - 1,)),
         ],
         compiler_params=pltpu.CompilerParams(
             collective_id=0, has_side_effects=True, vmem_limit_bytes=58 * 1024 * 1024
         ),
-    )(text_len, tile, pick, shift, peg_weight, prompt_rows[0], activation, modulation_weight, by_kind)
+    )(text_len, latents, pick, shift, peg_weight, prompt_rows[0], activation, modulation_weight, by_kind)
     return attended.reshape(1, frames, tile_h, tile_w * cols, head_width)
 
 
@@ -736,7 +792,7 @@
 
     def on_device(*blocks):
         group = blocks[4].shape[2] // rows
-        if items == 2 and cols % 2 == 0 and group >= 128 and group % 128 == 0 and blocks[0].shape[1:4] == (2, 4, 4):
+        if items == 2 and rows == 4 and cols % 2 == 0 and group >= 128 and group % 128 == 0 and blocks[0].shape[1:4] == (2, 4, 4):
             return on_device_fast(rows, cols, *blocks)
         return on_device_general(*blocks)
 

time: 51.6 us -> 53.3 us (1.033)
  Pallas kernels: 46.2 us -> 49.6 us
  local copies, waits for them, and re-layouts: 3.84 us -> 2.19 us
    pallas_call x1, Pallas kernels: 46.2 us -> 49.6 us  [on_device_fast(): pl.pallas_call(functools.partial(layer_kernel, (rows, cols, text, padded_...]
    reshape x1 -> x0, local copies, waits for them, and re-layouts: 1.65 us -> none  [on_device_fast(): tile = latents.reshape(tokens, width)]
where the time goes in v5:
time: 53.3 us; the launch traced here: 53.2 us
  Pallas kernels  49.6 us (93%)
  local copies, waits for them, and re-layouts  2.19 us (4%)
  between operations  1.32 us (2%)
    pallas_call x1, Pallas kernels, on_device_fast(): pl.pallas_call(functools.partial(layer_kernel, (rows, cols, text, padded_...  49.6 us
    unnamed x1, local copies, waits for them, and re-layouts  1.57 us

profile of v5, /device:TPU:0, one launch (start us, length us, event | category | flops | bytes accessed | tf_op | source)
XLA Modules:
  0.0 53.2 jit_solution(2837463428146983520)
XLA Ops:
  1.4 0.6 %broadcast_in_dim.2.act_ref = bf16[16,512]{1,0:T(8,128)(2,1)} broadcast(bf16[512]{0:T(512)(128)(2,1)S(1)} %fusion), dimensions={1} | broadcast | bytes 17408 | tf_op jit(solution)/shard_map/broadcast_in_dim | solution.py:709
  2.0 49.6 %shard_map.91 = bf16[128,512]{1,0:T(8,128)(2,1)} custom-call(s32[1]{0:T(128)S(6)} %copy.11.len_ref, bf16[1,2,4,4,3072]{4,3,2,1,0:T(4,128)(2,1)} %tile_ref.1, bf16[9,64,32]{2,1,0:T(8,128)(2,1)} %constant.12.clone.pick_ref, bf16[8,256,160]{2,1,0:T(8,128)(2,1)} %constant.13.clone.shift_hbm, bf16[3,3,3072]{2,1,0:T(4,128)(2,1)} %peg_ref.1, ...), custom_call_target="tpu_custom_call" | custom-call | tf_op jit(solution)/shard_map/pallas_call | solution.py:720
  51.6 1.6 %copy.13 = bf16[1,2,4,16,512]{4,3,2,1,0:T(8,128)(2,1)} copy(bf16[1,2,4,16,512]{4,3,2,1,0:T(8,128)(2,1)} %bitcast.6) | data formatting | bytes 262144
  (2 shorter events, 0.1 us)

commit v6 on v4

--- a/solution.py
+++ b/solution.py
@@ -219,6 +219,7 @@
     grid_x,
     send_text,
     recv_text,
+    tile_buf,
     own_text,
     send_part,
     recv_part,
@@ -243,7 +244,7 @@
     o_recv,
 ):
     rows, cols, text, padded_text, tile_w = sizes
-    tokens, width = tile_ref.shape
+    tokens, width = tile_buf.shape
     depth = weight_hbm.shape[1]
     out_w = weight_hbm.shape[2] // rows
     block = tokens * cols
@@ -302,7 +303,13 @@
     for step in range(1, cols):
         pl.semaphore_signal(barrier, inc=1, device_id={"col": col_peer(step)}, device_id_type=MESH)
 
-    tile = tile_ref[...]
+    pieces = [
+        tile_ref[0, f, h].astype(jnp.float32)
+        for f in range(tile_ref.shape[1])
+        for h in range(tile_ref.shape[2])
+    ]
+    tile_buf[...] = jnp.concatenate(pieces, axis=0).astype(jnp.bfloat16)
+    tile = tile_buf[...]
     wide = side_in.shape[2]
     narrow = corner_in.shape[1]
     edge = side_in.shape[1] // 2
@@ -362,16 +369,6 @@
         {"item": 1 - item},
     )
     weight_copy.start()
-    prompt_copy.wait()
-    text_stats = []
-    for start_row in range(0, padded_text, 16):
-        count = min(16, text - start_row)
-        values = prompt_ref[start_row : start_row + count, :].astype(jnp.float32)
-        center = jnp.mean(values, axis=-1, keepdims=True)
-        centered = values - center
-        spread = lax.rsqrt(jnp.mean(centered * centered, axis=-1, keepdims=True) + 1e-06)
-        text_stats.append((center, spread))
-
     for at, (down, right) in enumerate(SIDES):
 
         @pl.when(within(down, right))
@@ -438,39 +435,6 @@
             col, pl.ds(pl.multiple_of(row * tokens, tokens), tokens), order * depth : (order + 1) * depth
         ] = text_in[0:tokens, pl.ds(start, depth)]
 
-    weight_copy.wait_recv()
-
-    scale_pieces = [affine[1, :, pl.ds(start, depth)] for start in own_slices]
-    shift_pieces = [affine[0, :, pl.ds(start, depth)] for start in own_slices]
-    for start_row in range(0, padded_text, 16):
-        count = min(16, text - start_row)
-        center, spread = text_stats[start_row // 16]
-        for order, start in enumerate(own_slices):
-            part = prompt_ref[start_row : start_row + count, pl.ds(start, depth)].astype(jnp.float32)
-            normed = (part - center) * spread * scale_pieces[order] + shift_pieces[order]
-            if count < 16:
-                normed = jnp.concatenate([normed, jnp.zeros((16 - count, depth), jnp.float32)], axis=0)
-            text_in[start_row : start_row + 16, order * depth : (order + 1) * depth] = normed.astype(
-                jnp.bfloat16
-            )
-    text_values = text_in[:, 0 : 2 * depth]
-    t_copies = []
-    for step in range(1, rows):
-        peer = row_peer(step)
-        send_text[step - 1] = jnp.dot(
-            text_values, weights[peer, :, out_w:], preferred_element_type=jnp.float32
-        ).astype(jnp.bfloat16)
-        copy = remote(
-            send_text.at[step - 1],
-            recv_text.at[step - 1],
-            t_send.at[step - 1],
-            t_recv.at[step - 1],
-            {"row": peer},
-        )
-        copy.start()
-        t_copies.append(copy)
-    own_text[...] = jnp.dot(text_values, weights[row, :, out_w:], preferred_element_type=jnp.float32)
-
     for step in range(1, rows):
         source = lax.rem(row - step + rows, rows)
         remote(
@@ -525,6 +489,50 @@
             part_copy(group, step).start()
         own_part[group] = jnp.dot(values, weights[row], preferred_element_type=jnp.float32)
 
+    t_copies = []
+
+    def text_part():
+        prompt_copy.wait()
+        scale_pieces = [affine[1, :, pl.ds(start, depth)] for start in own_slices]
+        shift_pieces = [affine[0, :, pl.ds(start, depth)] for start in own_slices]
+        edges = list(range(0, text - text % 16, 64)) + [text - text % 16, text]
+        for first, last in zip(edges[:-1], edges[1:]):
+            if first == last:
+                continue
+            values = prompt_ref[first:last, :].astype(jnp.float32)
+            center = jnp.mean(values, axis=-1, keepdims=True)
+            centered = values - center
+            spread = lax.rsqrt(jnp.mean(centered * centered, axis=-1, keepdims=True) + 1e-06)
+            for order, start in enumerate(own_slices):
+                part = prompt_ref[first:last, pl.ds(start, depth)].astype(jnp.float32)
+                normed = (part - center) * spread * scale_pieces[order] + shift_pieces[order]
+                fill = -(last - first) % 16
+                if fill > 0:
+                    normed = jnp.concatenate([normed, jnp.zeros((fill, depth), jnp.float32)], axis=0)
+                text_in[first : last + fill, order * depth : (order + 1) * depth] = normed.astype(jnp.bfloat16)
+        filled = -(-text // 16) * 16
+        if filled < padded_text:
+            text_in[filled:padded_text, 0 : 2 * depth] = jnp.zeros(
+                (padded_text - filled, 2 * depth), jnp.bfloat16
+            )
+        text_values = text_in[0:padded_text, 0 : 2 * depth]
+        for step in range(1, rows):
+            peer = row_peer(step)
+            send_text[step - 1] = jnp.dot(
+                text_values, weights[peer, :, out_w:], preferred_element_type=jnp.float32
+            ).astype(jnp.bfloat16)
+            copy = remote(
+                send_text.at[step - 1],
+                recv_text.at[step - 1],
+                t_send.at[step - 1],
+                t_recv.at[step - 1],
+                {"row": peer},
+            )
+            copy.start()
+            t_copies.append(copy)
+        own_text[...] = jnp.dot(text_values, weights[row, :, out_w:], preferred_element_type=jnp.float32)
+
+    weight_copy.wait_recv()
     latent_part(col)
     for distance in range(1, cols):
         for direction in range(2):
@@ -540,6 +548,9 @@
             @pl.when(arrives(direction, distance))
             def multiply(direction=direction, distance=distance):
                 latent_part(col - distance * (1 - 2 * direction))
+
+        if distance == 1:
+            text_part()
 
     for copy in t_copies:
         copy.wait_recv()
@@ -571,35 +582,30 @@
     line = token // tile_w
     place = token - line * tile_w
     target = (line * cols + group) * tile_w + place
-    permute = jnp.where(at == target, 1.0, 0.0).astype(jnp.bfloat16)
+    permute = jnp.where(at == target, 0.125, 0.0).astype(jnp.bfloat16)
     keys = k_buf[...]
     vals = v_buf[...]
     position = lax.broadcasted_iota(jnp.int32, (1, keys.shape[0]), 1)
     valid = (position >= padded_text) | (position < len_ref[0])
+    head_of = lax.broadcasted_iota(jnp.int32, (1, out_w), 1) // HD
+    heads = out_w // HD
     o_copies = []
     for step in list(range(1, rows)) + [0]:
         peer = row_peer(step)
-        queries = jnp.dot(permute, q_buf[peer], preferred_element_type=jnp.float32).astype(jnp.bfloat16)
-        outs = []
-        for head in range(out_w // HD):
-            lanes = slice(head * HD, (head + 1) * HD)
-            scores = (
-                lax.dot_general(
-                    queries[:, lanes],
-                    keys[:, lanes],
-                    (((1,), (1,)), ((), ())),
-                    preferred_element_type=jnp.float32,
-                )
-                * 0.125
-            )
-            scores = jnp.where(valid, scores, -jnp.inf)
-            weight = jnp.exp(scores - jnp.max(scores, axis=-1, keepdims=True))
-            total = jnp.sum(weight, axis=-1, keepdims=True)
-            outs.append(
-                jnp.dot(weight.astype(jnp.bfloat16), vals[:, lanes], preferred_element_type=jnp.float32)
-                / total
-            )
-        result = jnp.concatenate(outs, axis=-1).astype(jnp.bfloat16)
+        queries = jnp.dot(permute, q_buf[peer], preferred_element_type=jnp.float32)
+        by_head = [jnp.where(head_of == head, queries, 0.0) for head in range(heads)]
+        stacked = jnp.concatenate(by_head, axis=0).astype(jnp.bfloat16)
+        scores = lax.dot_general(
+            stacked, keys, (((1,), (1,)), ((), ())), preferred_element_type=jnp.float32
+        )
+        scores = jnp.where(valid, scores, -jnp.inf)
+        weight = jnp.exp(scores - jnp.max(scores, axis=-1, keepdims=True))
+        total = jnp.sum(weight, axis=-1, keepdims=True)
+        mixed = jnp.dot(weight.astype(jnp.bfloat16), vals, preferred_element_type=jnp.float32) / total
+        result = mixed[0:block]
+        for head in range(1, heads):
+            result = jnp.where(head_of == head, mixed[head * block : (head + 1) * block], result)
+        result = result.astype(jnp.bfloat16)
         if step == 0:
             recv_out[row] = result
         else:
@@ -649,7 +655,6 @@
 ):
     frames, tile_h, tile_w, width = latents.shape[1:]
     tokens = frames * tile_h * tile_w
-    tile = latents.reshape(tokens, width)
     parts = 8
     narrow = width // parts
     pick, shift = (jnp.asarray(table, jnp.bfloat16) for table in halo_tables(frames, tile_h, tile_w, parts))
@@ -660,7 +665,7 @@
     out_w = head_width // rows
     by_kind = qkv_weight.transpose(1, 0, 2)
     text = prompt_rows.shape[1]
-    padded_text = -(-text // 16) * 16
+    padded_text = -(-text // 128) * 128
     block = tokens * cols
     group_rows = tokens * rows
     bf16, f32 = jnp.bfloat16, jnp.float32
@@ -691,6 +696,7 @@
             VMEM((cols, group_rows, 2 * depth), bf16),
             VMEM((rows - 1, padded_text, 2 * out_w), bf16),
             VMEM((rows - 1, padded_text, 2 * out_w), bf16),
+            VMEM((tokens, width), bf16),
             VMEM((padded_text, 2 * out_w), f32),
             VMEM((cols, rows - 1, group_rows, kinds * out_w), bf16),
             VMEM((cols, rows - 1, group_rows, kinds * out_w), bf16),
@@ -715,9 +721,9 @@
             dma((rows - 1,)),
         ],
         compiler_params=pltpu.CompilerParams(
-            collective_id=0, has_side_effects=True, vmem_limit_bytes=58 * 1024 * 1024
+            collective_id=0, has_side_effects=True, vmem_limit_bytes=52 * 1024 * 1024
         ),
-    )(text_len, tile, pick, shift, peg_weight, prompt_rows[0], activation, modulation_weight, by_kind)
+    )(text_len, latents, pick, shift, peg_weight, prompt_rows[0], activation, modulation_weight, by_kind)
     return attended.reshape(1, frames, tile_h, tile_w * cols, head_width)
 
 

time: 51.6 us -> 50.8 us (0.984)
  Pallas kernels: 46.2 us -> 44.6 us
  local copies, waits for them, and re-layouts: 3.84 us -> 4.61 us
    unnamed x1 -> x9, local copies, waits for them, and re-layouts: 1.57 us -> 4.6 us
    reshape x1 -> x0, local copies, waits for them, and re-layouts: 1.65 us -> none  [on_device_fast(): tile = latents.reshape(tokens, width)]
    pallas_call x1, Pallas kernels: 46.2 us -> 44.6 us  [on_device_fast(): pl.pallas_call(functools.partial(layer_kernel, (rows, cols, text, padded_...]
    broadcast_in_dim x1, local copies, waits for them, and re-layouts: 0.62 us -> 0.01 us  [on_device_fast(): activation = jnp.broadcast_to(activation[None, :], (16, temb))]
where the time goes in v6:
time: 50.8 us; the launch traced here: 50.6 us
  Pallas kernels  44.6 us (88%)
  local copies, waits for them, and re-layouts  4.61 us (9%)
  between operations  1.33 us (3%)
    pallas_call x1, Pallas kernels, on_device_fast(): pl.pallas_call(functools.partial(layer_kernel, (rows, cols, text, padded_...  44.6 us
    unnamed x9, local copies, waits for them, and re-layouts  4.6 us

profile of v6, /device:TPU:0, one launch (start us, length us, event | category | flops | bytes accessed | tf_op | source)
XLA Modules:
  0.0 50.6 jit_solution(4958397877409882694)
XLA Ops:
  1.4 0.0 copy-start
  1.4 1.2 %copy-done = bf16[8,256,160]{2,1,0:T(8,128)(2,1)S(1)} copy-done((bf16[8,256,160]{2,1,0:T(8,128)(2,1)S(1)}, bf16[8,256,160]{2,1,0:T(8,128)(2,1)}, u32[]{:S(2)}) %copy-start) | copy-done | bytes 655384
  2.6 0.0 copy-start.1
  2.6 0.9 %copy-done.1 = bf16[1,2,4,4,3072]{4,3,2,1,0:T(4,128)(2,1)S(1)} copy-done((bf16[1,2,4,4,3072]{4,3,2,1,0:T(4,128)(2,1)S(1)}, bf16[1,2,4,4,3072]{4,3,2,1,0:T(4,128)(2,1)}, u32[]{:S(2)}) %copy-start.1) | copy-done | bytes 196632
  3.5 0.0 copy-start.2
  3.5 0.9 %copy-done.2 = bf16[9,64,32]{2,1,0:T(8,128)(2,1)S(1)} copy-done((bf16[9,64,32]{2,1,0:T(8,128)(2,1)S(1)}, bf16[9,64,32]{2,1,0:T(8,128)(2,1)}, u32[]{:S(2)}) %copy-start.2) | copy-done | bytes 36888
  4.5 0.0 copy-start.3
  4.5 0.9 %copy-done.3 = bf16[3,3,3072]{2,1,0:T(4,128)(2,1)S(1)} copy-done((bf16[3,3,3072]{2,1,0:T(4,128)(2,1)S(1)}, bf16[3,3,3072]{2,1,0:T(4,128)(2,1)}, u32[]{:S(2)}) %copy-start.3) | copy-done | bytes 55320
  5.3 44.6 %shard_map.91 = bf16[128,512]{1,0:T(8,128)(2,1)S(1)} custom-call(s32[1]{0:T(128)S(6)} %copy.11.len_ref, bf16[1,2,4,4,3072]{4,3,2,1,0:T(4,128)(2,1)S(1)} %copy-done.1, bf16[9,64,32]{2,1,0:T(8,128)(2,1)S(1)} %copy-done.2, bf16[8,256,160]{2,1,0:T(8,128)(2,1)S(1)} %copy-done, bf16[3,3,3072]{2,1,0:T(4,128)(2,1)S(1)} %copy-done.3, bf16[226,3072]{1,0:T(8,128)(2,1)} %bitcast.5, ...), custom_call_target="tpu_custom_call" | custom-call | tf_op jit(solution)/shard_map/pallas_call | solution.py:674
  49.9 0.7 %copy.13 = bf16[1,2,4,16,512]{4,3,2,1,0:T(8,128)(2,1)} copy(bf16[1,2,4,16,512]{4,3,2,1,0:T(8,128)(2,1)S(1)} %bitcast.4) | data formatting | bytes 262144
  (3 shorter events, 0.1 us)
Async XLA Ops:
  1.4 1.2 %copy-start = (bf16[8,256,160]{2,1,0:T(8,128)(2,1)S(1)}, bf16[8,256,160]{2,1,0:T(8,128)(2,1)}, u32[]{:S(2)}) copy-start(bf16[8,256,160]{2,1,0:T(8,128)(2,1)} %constant.13.clone.shift_hbm) | copy-start | bytes 1966084
  2.6 0.9 %copy-start.1 = (bf16[1,2,4,4,3072]{4,3,2,1,0:T(4,128)(2,1)S(1)}, bf16[1,2,4,4,3072]{4,3,2,1,0:T(4,128)(2,1)}, u32[]{:S(2)}) copy-start(bf16[1,2,4,4,3072]{4,3,2,1,0:T(4,128)(2,1)} %tile_ref.1) | copy-start | bytes 589828
  3.5 0.9 %copy-start.2 = (bf16[9,64,32]{2,1,0:T(8,128)(2,1)S(1)}, bf16[9,64,32]{2,1,0:T(8,128)(2,1)}, u32[]{:S(2)}) copy-start(bf16[9,64,32]{2,1,0:T(8,128)(2,1)} %constant.12.clone.pick_ref) | copy-start | bytes 110596
  4.5 0.9 %copy-start.3 = (bf16[3,3,3072]{2,1,0:T(4,128)(2,1)S(1)}, bf16[3,3,3072]{2,1,0:T(4,128)(2,1)}, u32[]{:S(2)}) copy-start(bf16[3,3,3072]{2,1,0:T(4,128)(2,1)} %peg_ref.1) | copy-start | bytes 165892

commit v7 on v5

--- a/solution.py
+++ b/solution.py
@@ -548,12 +548,14 @@
             grid_x.at[source],
             z_send.at[direction, distance - 1],
             z_recv.at[direction, distance - 1],
-            {"col": col + sign},
+            {"col": col + sign * max(1, distance - 1)},
         )
 
     def passes(direction, distance):
-        home = col - (distance - 1) * (1 - 2 * direction)
-        return (home >= 0) & (home < cols) & (col < cols - 1 if direction == 0 else col > 0)
+        sign = 1 - 2 * direction
+        home = col - min(distance - 1, 1) * sign
+        target = col + max(1, distance - 1) * sign
+        return (home >= 0) & (home < cols) & (target >= 0) & (target < cols)
 
     def arrives(direction, distance):
         home = col - distance * (1 - 2 * direction)
@@ -564,7 +566,7 @@
 
             @pl.when(passes(direction, distance))
             def start(direction=direction):
-                z_copy(direction, distance, col - (distance - 1) * (1 - 2 * direction)).start()
+                z_copy(direction, distance, col - min(distance - 1, 1) * (1 - 2 * direction)).start()
 
     pass_on(1)
 
@@ -576,26 +578,27 @@
                 scatter_pass(col - distance * (1 - 2 * direction), *part_state)
 
     scatter_start(col, grid_x[col], 0, *part_state)
-    scatter_pass(0, *text_state)
     for distance in range(1, cols):
-        if distance == 1:
-            scatter_pass(col, *part_state)
-        else:
-            pass_sums(distance - 1)
         for direction in range(2):
 
             @pl.when(arrives(direction, distance))
             def landed(direction=direction, distance=distance):
                 z_copy(direction, distance, col - distance * (1 - 2 * direction)).wait_recv()
 
-        if distance < cols - 1:
-            pass_on(distance + 1)
+        if distance == 1:
+            pass_on(2)
+            pass_on(3)
+            scatter_pass(0, *text_state)
+            scatter_pass(col, *part_state)
         for direction in range(2):
 
             @pl.when(arrives(direction, distance))
             def multiply(direction=direction, distance=distance):
                 group = col - distance * (1 - 2 * direction)
                 scatter_start(group, grid_x[group], 0, *part_state)
+
+        if distance > 1:
+            pass_sums(distance - 1)
 
     pass_sums(cols - 1)
 
@@ -620,35 +623,30 @@
     line = token // tile_w
     place = token - line * tile_w
     target = (line * cols + group) * tile_w + place
-    permute = jnp.where(at == target, 1.0, 0.0).astype(jnp.bfloat16)
+    permute = jnp.where(at == target, 0.125, 0.0).astype(jnp.bfloat16)
     keys = k_buf[...]
     vals = v_buf[...]
     position = lax.broadcasted_iota(jnp.int32, (1, keys.shape[0]), 1)
     valid = (position >= padded_text) | (position < len_ref[0])
+    head_of = lax.broadcasted_iota(jnp.int32, (1, out_w), 1) // HD
+    heads = out_w // HD
     o_copies = []
     for step in list(range(1, rows)) + [0]:
         peer = row_peer(step)
-        queries = jnp.dot(permute, q_buf[peer], preferred_element_type=jnp.float32).astype(jnp.bfloat16)
-        outs = []
-        for head in range(out_w // HD):
-            lanes = slice(head * HD, (head + 1) * HD)
-            scores = (
-                lax.dot_general(
-                    queries[:, lanes],
-                    keys[:, lanes],
-                    (((1,), (1,)), ((), ())),
-                    preferred_element_type=jnp.float32,
-                )
-                * 0.125
-            )
-            scores = jnp.where(valid, scores, -jnp.inf)
-            weight = jnp.exp(scores - jnp.max(scores, axis=-1, keepdims=True))
-            total = jnp.sum(weight, axis=-1, keepdims=True)
-            outs.append(
-                jnp.dot(weight.astype(jnp.bfloat16), vals[:, lanes], preferred_element_type=jnp.float32)
-                / total
-            )
-        result = jnp.concatenate(outs, axis=-1).astype(jnp.bfloat16)
+        queries = jnp.dot(permute, q_buf[peer], preferred_element_type=jnp.float32)
+        by_head = [jnp.where(head_of == head, queries, 0.0) for head in range(heads)]
+        stacked = jnp.concatenate(by_head, axis=0).astype(jnp.bfloat16)
+        scores = lax.dot_general(
+            stacked, keys, (((1,), (1,)), ((), ())), preferred_element_type=jnp.float32
+        )
+        scores = jnp.where(valid, scores, -jnp.inf)
+        weight = jnp.exp(scores - jnp.max(scores, axis=-1, keepdims=True))
+        total = jnp.sum(weight, axis=-1, keepdims=True)
+        mixed = jnp.dot(weight.astype(jnp.bfloat16), vals, preferred_element_type=jnp.float32) / total
+        result = mixed[0:block]
+        for head in range(1, heads):
+            result = jnp.where(head_of == head, mixed[head * block : (head + 1) * block], result)
+        result = result.astype(jnp.bfloat16)
         if step == 0:
             recv_out[row] = result
         else:
@@ -684,7 +682,7 @@
 
             @pl.when(passes(direction, distance))
             def passed(direction=direction, distance=distance):
-                z_copy(direction, distance, col - (distance - 1) * (1 - 2 * direction)).wait_send()
+                z_copy(direction, distance, col - min(distance - 1, 1) * (1 - 2 * direction)).wait_send()
 
     for count, state in ((1, text_state), (cols, part_state)):
         own, first, first_in, hold, second, second_in, sems = state
@@ -792,7 +790,7 @@
 
     def on_device(*blocks):
         group = blocks[4].shape[2] // rows
-        if items == 2 and rows == 4 and cols % 2 == 0 and group >= 128 and group % 128 == 0 and blocks[0].shape[1:4] == (2, 4, 4):
+        if items == 2 and rows == 4 and cols == 4 and group >= 128 and group % 128 == 0 and blocks[0].shape[1:4] == (2, 4, 4):
             return on_device_fast(rows, cols, *blocks)
         return on_device_general(*blocks)
 

time: 53.3 us -> 50.7 us (0.951)
  Pallas kernels: 49.6 us -> 47 us
    pallas_call x1, Pallas kernels: 49.6 us -> 47 us  [on_device_fast(): pl.pallas_call(functools.partial(layer_kernel, (rows, cols, text, padded_...]
where the time goes in v7:
time: 50.7 us; the launch traced here: 50.6 us
  Pallas kernels  47 us (93%)
  local copies, waits for them, and re-layouts  2.19 us (4%)
  between operations  1.32 us (3%)
    pallas_call x1, Pallas kernels, on_device_fast(): pl.pallas_call(functools.partial(layer_kernel, (rows, cols, text, padded_...  47 us
    unnamed x1, local copies, waits for them, and re-layouts  1.57 us

profile of v7, /device:TPU:0, one launch (start us, length us, event | category | flops | bytes accessed | tf_op | source)
XLA Modules:
  0.0 50.6 jit_solution(7817643208090130772)
XLA Ops:
  1.4 0.6 %broadcast_in_dim.2.act_ref = bf16[16,512]{1,0:T(8,128)(2,1)} broadcast(bf16[512]{0:T(512)(128)(2,1)S(1)} %fusion), dimensions={1} | broadcast | bytes 17408 | tf_op jit(solution)/shard_map/broadcast_in_dim | solution.py:707
  2.0 47.0 %shard_map.91 = bf16[128,512]{1,0:T(8,128)(2,1)} custom-call(s32[1]{0:T(128)S(6)} %copy.11.len_ref, bf16[1,2,4,4,3072]{4,3,2,1,0:T(4,128)(2,1)} %tile_ref.1, bf16[9,64,32]{2,1,0:T(8,128)(2,1)} %constant.12.clone.pick_ref, bf16[8,256,160]{2,1,0:T(8,128)(2,1)} %constant.13.clone.shift_hbm, bf16[3,3,3072]{2,1,0:T(4,128)(2,1)} %peg_ref.1, ...), custom_call_target="tpu_custom_call" | custom-call | tf_op jit(solution)/shard_map/pallas_call | solution.py:718
  49.0 1.6 %copy.13 = bf16[1,2,4,16,512]{4,3,2,1,0:T(8,128)(2,1)} copy(bf16[1,2,4,16,512]{4,3,2,1,0:T(8,128)(2,1)} %bitcast.6) | data formatting | bytes 262144
  (2 shorter events, 0.1 us)

commit v8 on v7

--- a/solution.py
+++ b/solution.py
@@ -433,18 +433,6 @@
         {"item": 1 - item},
     )
     weight_copy.start()
-    prompt_copy.wait()
-    text_stats = []
-    for start_row in range(0, padded_text, 16):
-        count = min(16, text - start_row)
-        if count <= 0:
-            continue
-        values = prompt_ref[start_row : start_row + count, :].astype(jnp.float32)
-        center = jnp.mean(values, axis=-1, keepdims=True)
-        centered = values - center
-        spread = lax.rsqrt(jnp.mean(centered * centered, axis=-1, keepdims=True) + 1e-06)
-        text_stats.append((center, spread))
-
     for at, (down, right) in enumerate(SIDES):
 
         @pl.when(within(down, right))
@@ -511,27 +499,6 @@
             col, pl.ds(pl.multiple_of(row * tokens, tokens), tokens), order * depth : (order + 1) * depth
         ] = text_in[0:tokens, pl.ds(start, depth)]
 
-    weight_copy.wait_recv()
-
-    scale_pieces = [affine[1, :, pl.ds(start, depth)] for start in own_slices]
-    shift_pieces = [affine[0, :, pl.ds(start, depth)] for start in own_slices]
-    for start_row in range(0, padded_text, 16):
-        count = min(16, text - start_row)
-        if count <= 0:
-            text_in[start_row : start_row + 16, 0 : 2 * depth] = jnp.zeros((16, 2 * depth), jnp.bfloat16)
-            continue
-        center, spread = text_stats[start_row // 16]
-        for order, start in enumerate(own_slices):
-            part = prompt_ref[start_row : start_row + count, pl.ds(start, depth)].astype(jnp.float32)
-            normed = (part - center) * spread * scale_pieces[order] + shift_pieces[order]
-            if count < 16:
-                normed = jnp.concatenate([normed, jnp.zeros((16 - count, depth), jnp.float32)], axis=0)
-            text_in[start_row : start_row + 16, order * depth : (order + 1) * depth] = normed.astype(
-                jnp.bfloat16
-            )
-    text_values = text_in[:, 0 : 2 * depth]
-    scatter_start(0, text_values, out_w, *text_state)
-
     for step in range(1, rows):
         source = lax.rem(row - step + rows, rows)
         remote(
@@ -577,6 +544,39 @@
             def forward(direction=direction):
                 scatter_pass(col - distance * (1 - 2 * direction), *part_state)
 
+    def text_part():
+        prompt_copy.wait()
+        text_stats = []
+        for start_row in range(0, padded_text, 16):
+            count = min(16, text - start_row)
+            if count <= 0:
+                continue
+            values = prompt_ref[start_row : start_row + count, :].astype(jnp.float32)
+            center = jnp.mean(values, axis=-1, keepdims=True)
+            centered = values - center
+            spread = lax.rsqrt(jnp.mean(centered * centered, axis=-1, keepdims=True) + 1e-06)
+            text_stats.append((center, spread))
+
+        scale_pieces = [affine[1, :, pl.ds(start, depth)] for start in own_slices]
+        shift_pieces = [affine[0, :, pl.ds(start, depth)] for start in own_slices]
+        for start_row in range(0, padded_text, 16):
+            count = min(16, text - start_row)
+            if count <= 0:
+                text_in[start_row : start_row + 16, 0 : 2 * depth] = jnp.zeros((16, 2 * depth), jnp.bfloat16)
+                continue
+            center, spread = text_stats[start_row // 16]
+            for order, start in enumerate(own_slices):
+                part = prompt_ref[start_row : start_row + count, pl.ds(start, depth)].astype(jnp.float32)
+                normed = (part - center) * spread * scale_pieces[order] + shift_pieces[order]
+                if count < 16:
+                    normed = jnp.concatenate([normed, jnp.zeros((16 - count, depth), jnp.float32)], axis=0)
+                text_in[start_row : start_row + 16, order * depth : (order + 1) * depth] = normed.astype(
+                    jnp.bfloat16
+                )
+        text_values = text_in[:, 0 : 2 * depth]
+        scatter_start(0, text_values, out_w, *text_state)
+
+    weight_copy.wait_recv()
     scatter_start(col, grid_x[col], 0, *part_state)
     for distance in range(1, cols):
         for direction in range(2):
@@ -588,7 +588,6 @@
         if distance == 1:
             pass_on(2)
             pass_on(3)
-            scatter_pass(0, *text_state)
             scatter_pass(col, *part_state)
         for direction in range(2):
 
@@ -597,8 +596,12 @@
                 group = col - distance * (1 - 2 * direction)
                 scatter_start(group, grid_x[group], 0, *part_state)
 
-        if distance > 1:
+        if distance == 1:
+            text_part()
+        else:
             pass_sums(distance - 1)
+        if distance == 2:
+            scatter_pass(0, *text_state)
 
     pass_sums(cols - 1)
 

time: 50.7 us -> 50.9 us (level)
  no operation moved by 1% of the time
where the time goes in v8:
time: 50.9 us; the launch traced here: 50.8 us
  Pallas kernels  47.2 us (93%)
  local copies, waits for them, and re-layouts  2.19 us (4%)
  between operations  1.32 us (3%)
    pallas_call x1, Pallas kernels, on_device_fast(): pl.pallas_call(functools.partial(layer_kernel, (rows, cols, text, padded_...  47.2 us
    unnamed x1, local copies, waits for them, and re-layouts  1.57 us

profile of v8, /device:TPU:0, one launch (start us, length us, event | category | flops | bytes accessed | tf_op | source)
XLA Modules:
  0.0 50.8 jit_solution(14857845713289092849)
XLA Ops:
  1.4 0.6 %broadcast_in_dim.2.act_ref = bf16[16,512]{1,0:T(8,128)(2,1)} broadcast(bf16[512]{0:T(512)(128)(2,1)S(1)} %fusion), dimensions={1} | broadcast | bytes 17408 | tf_op jit(solution)/shard_map/broadcast_in_dim | solution.py:710
  2.0 47.2 %shard_map.91 = bf16[128,512]{1,0:T(8,128)(2,1)} custom-call(s32[1]{0:T(128)S(6)} %copy.11.len_ref, bf16[1,2,4,4,3072]{4,3,2,1,0:T(4,128)(2,1)} %tile_ref.1, bf16[9,64,32]{2,1,0:T(8,128)(2,1)} %constant.12.clone.pick_ref, bf16[8,256,160]{2,1,0:T(8,128)(2,1)} %constant.13.clone.shift_hbm, bf16[3,3,3072]{2,1,0:T(4,128)(2,1)} %peg_ref.1, ...), custom_call_target="tpu_custom_call" | custom-call | tf_op jit(solution)/shard_map/pallas_call | solution.py:721
  49.2 1.6 %copy.13 = bf16[1,2,4,16,512]{4,3,2,1,0:T(8,128)(2,1)} copy(bf16[1,2,4,16,512]{4,3,2,1,0:T(8,128)(2,1)} %bitcast.6) | data formatting | bytes 262144
  (2 shorter events, 0.1 us)
